TPU v7x, 32 devices: a whole 2x2x4 slice. The times are simulated.
32 devices in a mesh: blk: 16 (over z, y, x), grp: 2 (over core).
Axes of the slice: x: 2, y: 2, z: 4, core: 2. Of those that a mesh axis runs over, the one named last changes fastest.
Arguments:
- samples: float32 [32, 1024], P(None, ('blk', 'grp')), may hold values from 0 to 256
- bounds: int32 [2, 32, 2048], P(None, None, 'blk'), may hold values from 0 to 256, as said below
- spread: float32 [32], replicated, may hold values from 2 to 8
- counts: int32 [2048], P('blk'), may hold values from 0 to 2047
Outputs:
- log_estimate: float32 [2048], P('blk')
- spread_grad: float32 [32], replicated
Inputs may be any that keep to these rules, and one draw needn't show every extreme that they name: For every query and dimension bounds[0] < bounds[1]; each query restricts exactly 3 dimensions to a width of 16 to 48 cells and has bounds 0 and 256 in all others.
All inputs are finite; a program needn't handle non-finite values.
Results may differ from a plain program's by a relative error of at most 0.0003.
Values sent between devices are 32-bit elements; how exact they have to be, the bound alone decides.
No kernel may reach another device: no remote copies, remote signals or barrier semaphores. Data moves between devices by JAX's collectives and lax.ppermute only.
A program may use at most 64 MiB of HBM per device.

v0:
```python
import functools

import jax
import jax.numpy as jnp
from jax import lax
from jax.experimental import pallas as pl
from jax.experimental.pallas import tpu as pltpu
from jax.sharding import PartitionSpec as P

TABLE_ROWS = 1048576
GRID = 256
LIMITED = 3

ROOT_HALF = 0.7071067811865476
LOG2_E = 1.4426950408889634
SLOPE = 0.5641895835477563


def box_terms(low, high):
    low_bell = jnp.exp2((low * low) * -LOG2_E)
    high_bell = jnp.exp2((high * high) * -LOG2_E)
    return lax.erf(high) - lax.erf(low), low * low_bell - high * high_bell


def split(x, parts):
    out = []
    for _ in range(parts - 1):
        head = x.astype(jnp.bfloat16)
        out.append(head)
        x = x - head.astype(jnp.float32)
    return out + [x.astype(jnp.bfloat16)]


def tree_sum(parts):
    while len(parts) > 1:
        parts = [a + b for a, b in zip(parts[::2], parts[1::2])]
    return parts[0]


def load_kernel(
    x_ref, bounds_ref, spread_ref, counts_ref,
    out_ref, held_bounds, held_spread, target_ref,
    held_x, held_counts, sems,
):
    sources = (x_ref, bounds_ref, spread_ref, counts_ref)
    targets = (held_x, held_bounds, held_spread, held_counts)
    copies = [
        pltpu.make_async_copy(source, target, sems.at[i])
        for i, (source, target) in enumerate(zip(sources, targets))
    ]
    for copy in copies:
        copy.start()
    copies[0].wait()
    rows = held_x.shape[0]
    packed = jnp.concatenate([held_x[8 * j : 8 * (j + 1), :] for j in range(rows // 8)], axis=1)
    for peer in range(out_ref.shape[0]):
        out_ref[peer] = packed
    for copy in copies[1:]:
        copy.wait()
    smoothing = 1.0 / TABLE_ROWS
    target_ref[...] = jnp.log(held_counts[...].astype(jnp.float32) / TABLE_ROWS + smoothing)


def terms_kernel(width, blocks_ref, bounds_ref, spread_ref, out_ref):
    dims, queries = bounds_ref.shape[1:]
    count = blocks_ref.shape[0]
    per_piece = 128 // width
    group = min(count, 4 * per_piece)

    low, high = bounds_ref[0], bounds_ref[1]
    limited = (high - low) != GRID
    at = lax.broadcasted_iota(jnp.int32, (dims, queries), 0)
    first = jnp.min(jnp.where(limited, at, dims), axis=0, keepdims=True)
    last = jnp.max(jnp.where(limited, at, -1), axis=0, keepdims=True)
    chosen = [at == first, limited & (at > first) & (at < last), at == last]

    row = lax.broadcasted_iota(jnp.int32, (dims, dims), 0)
    column = lax.broadcasted_iota(jnp.int32, (dims, dims), 1)
    spread = jnp.sum(jnp.where(row == column, spread_ref[...], 0.0), axis=1, keepdims=True)
    unit = ROOT_HALF / spread

    pick = lambda mask, values: jnp.sum(jnp.where(mask, values, 0.0), axis=0, keepdims=True)
    low = low.astype(jnp.float32) * unit
    high = high.astype(jnp.float32) * unit
    low_at = [pick(mask, low) for mask in chosen]
    high_at = [pick(mask, high) for mask in chosen]

    ones = [mask.astype(jnp.float32).astype(jnp.bfloat16) for mask in chosen]
    free = jnp.where(limited, 0.0, 1.0).astype(jnp.bfloat16)
    none = jnp.zeros_like(free)
    right = jnp.concatenate(
        [jnp.concatenate(ones + [none], axis=1)] * 3
        + [jnp.concatenate([none] * LIMITED + [free], axis=1)] * 3,
        axis=0,
    )

    def step(picked, sums):
        others = jnp.exp2(picked[:, LIMITED * queries :])
        mass, slope = [], []
        for k in range(LIMITED):
            points = picked[:, k * queries : (k + 1) * queries]
            m, s = box_terms(low_at[k] - points, high_at[k] - points)
            mass.append(m)
            slope.append(s)
        pair = others * mass[0]
        last_two = pair * mass[1]
        whole = last_two * mass[2]
        return whole, (
            sums[0] + whole,
            sums[1] + (others * mass[1]) * (mass[2] * slope[0]),
            sums[2] + pair * (mass[2] * slope[1]),
            sums[3] + last_two * slope[2],
        )

    def piece(start, totals):
        sums, products = totals[:-1], totals[-1]
        some = [blocks_ref[start + b] for b in range(per_piece)]
        x = unit * jnp.concatenate(
            [
                jnp.concatenate([block[:, width * j : width * (j + 1)] for block in some], axis=1)
                for j in range(dims // 8)
            ],
            axis=0,
        )
        full, slope = box_terms(-x, float(GRID) * unit - x)
        ratio = jnp.concatenate(split(slope / full, 2), axis=0)
        left = jnp.concatenate(split(x, 3) + split(jnp.log(0.5 * full) * LOG2_E, 3), axis=0)
        picked = lax.dot_general(
            left, right, (((0,), (0,)), ((), ())), preferred_element_type=jnp.float32
        )
        inside = []
        for at_row in range(0, per_piece * width, 16):
            whole, sums = step(picked[at_row : at_row + 16], sums)
            inside.append(jnp.concatenate(split(whole, 2), axis=1))
        inside = jnp.concatenate(inside, axis=0)
        products = products + jnp.dot(ratio, inside, preferred_element_type=jnp.float32)
        return (*sums, products)

    def pieces(number, totals):
        for start in range(0, group, per_piece):
            totals = piece(number * group + start, totals)
        return totals

    zero = jnp.zeros((16, queries), jnp.float32)
    totals = (zero,) * (1 + LIMITED) + (jnp.zeros((2 * dims, 2 * queries), jnp.float32),)
    if count == group:
        totals = pieces(0, totals)
    else:
        totals = lax.fori_loop(0, count // group, pieces, totals)
    sums = [jnp.sum(s, axis=0, keepdims=True) for s in totals[:-1]]
    products = totals[-1]
    deriv = products[:dims, :queries] + (products[dims:, :queries] + products[:dims, queries:])
    deriv = jnp.where(limited, 0.0, deriv * (SLOPE / 4))
    for mask, s in zip(chosen, sums[1:]):
        deriv = jnp.where(mask, s * (SLOPE / 4), deriv)
    out_ref[:dims, :] = deriv
    out_ref[dims:, :] = jnp.broadcast_to(sums[0] * 0.125, (8, queries))


def finish_kernel(sample_total, query_total, *refs):
    part_refs, (target_ref, log_ref, share_ref) = refs[:-3], refs[-3:]
    whole = tree_sum([ref[...] for ref in part_refs])
    dims, queries = whole.shape[0] - 8, whole.shape[1]
    smoothing = 1.0 / TABLE_ROWS
    estimate = whole[dims : dims + 1] / sample_total
    log_est = jnp.log(estimate + smoothing)
    log_ref[...] = log_est
    weight = 2.0 * (log_est - target_ref[...]) / (query_total * (estimate + smoothing))
    terms = whole[:dims] * (weight / sample_total)
    terms = jnp.concatenate([terms, jnp.zeros((queries - dims, queries), jnp.float32)], axis=0)
    share = jnp.sum(terms.T, axis=0, keepdims=True)
    for peer in range(share_ref.shape[0]):
        share_ref[peer] = share


def last_kernel(shares_ref, held_log_ref, log_ref, gradient_ref):
    total = tree_sum([shares_ref[peer] for peer in range(shares_ref.shape[0])])
    log_ref[...] = held_log_ref[0]
    gradient_ref[...] = total[0, : gradient_ref.shape[0]]


def everyone(x, axis):
    size = lax.axis_size(axis)
    return [x] + [
        lax.ppermute(x, axis, [(i, i ^ offset) for i in range(size)]) for offset in range(1, size)
    ]


def call(kernel, args, outs, scratch=(), placed=pltpu.VMEM):
    single = len(outs) == 1
    return pl.pallas_call(
        kernel,
        out_shape=outs[0] if single else outs,
        in_specs=[pl.BlockSpec(memory_space=placed)] * len(args),
        out_specs=pl.BlockSpec(memory_space=pltpu.VMEM)
        if single
        else [pl.BlockSpec(memory_space=pltpu.VMEM)] * len(outs),
        scratch_shapes=list(scratch),
        compiler_params=pltpu.CompilerParams(vmem_limit_bytes=32 << 20),
    )(*args)


def shape(*sizes):
    return jax.ShapeDtypeStruct(sizes, jnp.float32)


def on_device(samples, bounds, spread, counts):
    dims, width = samples.shape
    queries = bounds.shape[2]
    blocks, copies = lax.axis_size("blk"), lax.axis_size("grp")
    sample_total = width * blocks * copies
    query_total = queries * blocks

    counts_vector = pltpu.VMEM((1, queries), jnp.int32)
    packed, bounds, spread, target = call(
        load_kernel,
        [
            pltpu.with_memory_space_constraint(array, pltpu.HBM)
            for array in (samples, bounds, spread.reshape(1, dims), counts.reshape(1, queries))
        ],
        [
            pltpu.VMEM((blocks, 8, dims * width // 8), jnp.float32),
            pltpu.VMEM(bounds.shape, bounds.dtype),
            pltpu.VMEM((1, dims), jnp.float32),
            pltpu.VMEM((1, queries), jnp.float32),
        ],
        [pltpu.VMEM((dims, width), jnp.float32), counts_vector, pltpu.SemaphoreType.DMA((4,))],
        placed=pl.ANY,
    )
    order = [list(reversed(range(blocks)))]
    gathered = lax.all_to_all(packed, "blk", 0, 0, axis_index_groups=order)
    part = call(
        functools.partial(terms_kernel, width),
        [gathered, bounds, spread],
        [shape(dims + 8, queries)],
    )
    log_est, share = call(
        functools.partial(finish_kernel, sample_total, query_total),
        everyone(part, "grp") + [target],
        [shape(1, queries), shape(blocks, 1, queries)],
    )
    shares = lax.all_to_all(share, "blk", 0, 0, axis_index_groups=order)
    return call(last_kernel, [shares, log_est], [shape(queries), shape(dims)])


def solution(mesh):
    return jax.shard_map(
        on_device,
        mesh=mesh,
        in_specs=(P(None, ("blk", "grp")), P(None, None, "blk"), P(), P("blk")),
        out_specs=(P("blk"), P()),
        check_vma=False,
    )
```

profile of v0, /device:TPU:0, one launch (start us, length us, event | category | flops | bytes accessed | tf_op | source)
XLA Modules:
  0.0 26.2 jit_solution(744266800034772267)
XLA Ops:
  0.6 0.8 %shard_map.59 = (f32[16,8,128]{2,1,0:T(8,128)S(1)}, s32[2,32,128]{2,1,0:T(8,128)S(1)}, f32[1,32]{1,0:T(1,128)S(1)}, f32[1,128]{1,0:T(1,128)S(1)}) custom-call(f32[32,32]{1,0:T(8,128)} %x_ref.1, s32[2,32,128]{2,1,0:T(8,128)} %bounds_ref.1, f32[1,32]{1,0:T(1,128)} %bitcast.2, s32[1,128]{1,0:T(1,128)} %bitcast.3), custom_call_target="tpu_custom_call" | custom-call | tf_op jit(solution)/shard_map/pallas_call | solution.py:191
  1.5 12.3 %all_to_all.10.blocks_ref = f32[16,8,128]{2,1,0:T(8,128)S(1)} all-to-all(f32[16,8,128]{2,1,0:T(8,128)S(1)} %get-tuple-element.8), channel_id=1, replica_groups={{30,28,26,24,22,20,18,16,14,12,10,8,6,4,2,0},{31,29,27,25,23,21,19,17,1..., dimensions={0} | all-to-all | bytes 131072 | tf_op jit(solution)/shard_map/all_to_all | solution.py:231
  13.8 1.0 %shard_map.60.refs_0_ = f32[40,128]{1,0:T(8,128)S(1)} custom-call(f32[16,8,128]{2,1,0:T(8,128)S(1)} %all_to_all.10.blocks_ref, s32[2,32,128]{2,1,0:T(8,128)S(1)} %get-tuple-element.9.bounds_ref, f32[1,32]{1,0:T(1,128)S(1)} %get-tuple-element.10.spread_ref), custom_call_target="tpu_custom_call" | custom-call | tf_op jit(solution)/shard_map/pallas_call | solution.py:191
  14.8 0.1 collective-permute-start
  14.9 1.2 %collective-permute-done.refs_1_ = f32[40,128]{1,0:T(8,128)S(1)} collective-permute-done((f32[40,128]{1,0:T(8,128)S(1)}, f32[40,128]{1,0:T(8,128)S(1)}, u32[]{:S(2)}, u32[]{:S(2)}) %collective-permute-start) | collective-permute-done | bytes 20512 | tf_op jit(solution)/shard_map/ppermute | solution.py:185
  16.1 0.1 shard_map.61
  16.2 9.5 %all_to_all.11.shares_ref = f32[16,1,128]{2,1,0:T(1,128)S(1)} all-to-all(f32[16,1,128]{2,1,0:T(1,128)S(1)} %get-tuple-element.12), channel_id=1, replica_groups={{30,28,26,24,22,20,18,16,14,12,10,8,6,4,2,0},{31,29,27,25,23,21,19,17,1..., dimensions={0} | all-to-all | bytes 16384 | tf_op jit(solution)/shard_map/all_to_all | solution.py:242
  25.7 0.5 %shard_map.62 = (f32[128]{0:T(128)}, f32[32]{0:T(128)}) custom-call(f32[16,1,128]{2,1,0:T(1,128)S(1)} %all_to_all.11.shares_ref, f32[1,128]{1,0:T(1,128)S(1)} %get-tuple-element.13.held_log_ref), custom_call_target="tpu_custom_call" | custom-call | tf_op jit(solution)/shard_map/pallas_call | solution.py:191
Async XLA Ops:
  14.8 1.3 %collective-permute-start = (f32[40,128]{1,0:T(8,128)S(1)}, f32[40,128]{1,0:T(8,128)S(1)}, u32[]{:S(2)}, u32[]{:S(2)}) collective-permute-start(f32[40,128]{1,0:T(8,128)S(1)} %shard_map.60.refs_0_), channel_id=1, source_target_pairs={{0,1},{1,0},{2,3},{3,2},{4,5},{5,4},{6,7},{7,6},{8,9},{9,8},{10,11... | collective-permute-start | bytes 61448 | tf_op jit(solution)/shard_map/ppermute | solution.py:185
where the time goes:
time: 26.5 us; the launch traced here: 26.2 us
  blocking collectives  21.8 us (82%)
  Pallas kernels  2.49 us (9%)
  waiting for transfers between devices  1.18 us (4%)
  between operations  0.66 us (2%)
    all_to_all x1, blocking collectives, on_device(): gathered = lax.all_to_all(packed, 'blk', 0, 0, axis_index_groups=order)  12.3 us
    all_to_all x1, blocking collectives, on_device(): shares = lax.all_to_all(share, 'blk', 0, 0, axis_index_groups=order)  9.5 us
    pallas_call x4, Pallas kernels, call(): pl.pallas_call(kernel, out_shape=outs[0] if single else outs, in_specs=[p...  2.49 us
    ppermute x1, waiting for transfers between devices, everyone(): lax.ppermute(x, axis, [(i, i ^ offset) for i in range(size)])  1.18 us
  transfers between devices with their start and end apart: 1, of which 1 were waited for; matrix products, arithmetic and copies ran while one was open for 0% of the time, Pallas kernels for 0%

commit v1 on v0

--- a/solution.py
+++ b/solution.py
@@ -227,8 +227,13 @@
         [pltpu.VMEM((dims, width), jnp.float32), counts_vector, pltpu.SemaphoreType.DMA((4,))],
         placed=pl.ANY,
     )
-    order = [list(reversed(range(blocks)))]
-    gathered = lax.all_to_all(packed, "blk", 0, 0, axis_index_groups=order)
+    turned = [1] + [0] * (blocks - 1)
+    groups = [
+        [b * copies + (c + turned[b]) % copies for b in reversed(range(blocks))]
+        for c in range(copies)
+    ]
+    exchange = lambda x: lax.all_to_all(x, ("blk", "grp"), 0, 0, axis_index_groups=groups)
+    gathered = exchange(packed)
     part = call(
         functools.partial(terms_kernel, width),
         [gathered, bounds, spread],
@@ -239,7 +244,7 @@
         everyone(part, "grp") + [target],
         [shape(1, queries), shape(blocks, 1, queries)],
     )
-    shares = lax.all_to_all(share, "blk", 0, 0, axis_index_groups=order)
+    shares = exchange(share)
     return call(last_kernel, [shares, log_est], [shape(queries), shape(dims)])
 
 

time: 26.5 us -> 25.6 us (0.966)
  blocking collectives: 21.8 us -> 20.1 us
  starting transfers between devices: 0.07 us -> 1.01 us
  waiting for transfers between devices: 1.18 us -> 0.84 us
    all_to_all x2, blocking collectives: 21.8 us -> 20.1 us  [on_device(): lax.all_to_all(x, ('blk', 'grp'), 0, 0, axis_index_groups=groups)]
    ppermute x1, starting transfers between devices: 0.07 us -> 1.01 us  [everyone(): lax.ppermute(x, axis, [(i, i ^ offset) for i in range(size)])]
    ppermute x1, waiting for transfers between devices: 1.18 us -> 0.84 us  [everyone(): lax.ppermute(x, axis, [(i, i ^ offset) for i in range(size)])]
where the time goes in v1:
time: 25.6 us; the launch traced here: 25.1 us
  blocking collectives  20.1 us (79%)
  Pallas kernels  2.49 us (10%)
  starting transfers between devices  1.01 us (4%)
  waiting for transfers between devices  0.84 us (3%)
  between operations  0.66 us (3%)
    all_to_all x2, blocking collectives, on_device(): lax.all_to_all(x, ('blk', 'grp'), 0, 0, axis_index_groups=groups)  20.1 us
    pallas_call x4, Pallas kernels, call(): pl.pallas_call(kernel, out_shape=outs[0] if single else outs, in_specs=[p...  2.49 us
    ppermute x1, starting transfers between devices, everyone(): lax.ppermute(x, axis, [(i, i ^ offset) for i in range(size)])  1.01 us
    ppermute x1, waiting for transfers between devices, everyone(): lax.ppermute(x, axis, [(i, i ^ offset) for i in range(size)])  0.84 us
  transfers between devices with their start and end apart: 1, of which 1 were waited for; matrix products, arithmetic and copies ran while one was open for 0% of the time, Pallas kernels for 0%

profile of v1, /device:TPU:0, one launch (start us, length us, event | category | flops | bytes accessed | tf_op | source)
XLA Modules:
  0.0 25.1 jit_solution(1073707012866403314)
XLA Ops:
  0.6 0.8 %shard_map.59 = (f32[16,8,128]{2,1,0:T(8,128)S(1)}, s32[2,32,128]{2,1,0:T(8,128)S(1)}, f32[1,32]{1,0:T(1,128)S(1)}, f32[1,128]{1,0:T(1,128)S(1)}) custom-call(f32[32,32]{1,0:T(8,128)} %x_ref.1, s32[2,32,128]{2,1,0:T(8,128)} %bounds_ref.1, f32[1,32]{1,0:T(1,128)} %bitcast.2, s32[1,128]{1,0:T(1,128)} %bitcast.3), custom_call_target="tpu_custom_call" | custom-call | tf_op jit(solution)/shard_map/pallas_call | solution.py:191
  1.5 11.2 %all_to_all.10.blocks_ref = f32[16,8,128]{2,1,0:T(8,128)S(1)} all-to-all(f32[16,8,128]{2,1,0:T(8,128)S(1)} %get-tuple-element.8), channel_id=1, replica_groups={{30,28,26,24,22,20,18,16,14,12,10,8,6,4,2,1},{31,29,27,25,23,21,19,17,1..., dimensions={0} | all-to-all | bytes 131072 | tf_op jit(solution)/shard_map/all_to_all | solution.py:235
  12.7 1.0 %shard_map.60.refs_0_ = f32[40,128]{1,0:T(8,128)S(1)} custom-call(f32[16,8,128]{2,1,0:T(8,128)S(1)} %all_to_all.10.blocks_ref, s32[2,32,128]{2,1,0:T(8,128)S(1)} %get-tuple-element.9.bounds_ref, f32[1,32]{1,0:T(1,128)S(1)} %get-tuple-element.10.spread_ref), custom_call_target="tpu_custom_call" | custom-call | tf_op jit(solution)/shard_map/pallas_call | solution.py:191
  13.7 1.0 %collective-permute-start = (f32[40,128]{1,0:T(8,128)S(1)}, f32[40,128]{1,0:T(8,128)S(1)}, u32[]{:S(2)}, u32[]{:S(2)}) collective-permute-start(f32[40,128]{1,0:T(8,128)S(1)} %shard_map.60.refs_0_), channel_id=1, source_target_pairs={{0,1},{1,0},{2,3},{3,2},{4,5},{5,4},{6,7},{7,6},{8,9},{9,8},{10,11... | collective-permute-start | bytes 61448 | tf_op jit(solution)/shard_map/ppermute | solution.py:185
  14.7 0.8 %collective-permute-done.refs_1_ = f32[40,128]{1,0:T(8,128)S(1)} collective-permute-done((f32[40,128]{1,0:T(8,128)S(1)}, f32[40,128]{1,0:T(8,128)S(1)}, u32[]{:S(2)}, u32[]{:S(2)}) %collective-permute-start) | collective-permute-done | bytes 20512 | tf_op jit(solution)/shard_map/ppermute | solution.py:185
  15.6 0.1 shard_map.61
  15.7 8.9 %all_to_all.11.shares_ref = f32[16,1,128]{2,1,0:T(1,128)S(1)} all-to-all(f32[16,1,128]{2,1,0:T(1,128)S(1)} %get-tuple-element.12), channel_id=1, replica_groups={{30,28,26,24,22,20,18,16,14,12,10,8,6,4,2,1},{31,29,27,25,23,21,19,17,1..., dimensions={0} | all-to-all | bytes 16384 | tf_op jit(solution)/shard_map/all_to_all | solution.py:235
  24.6 0.5 %shard_map.62 = (f32[128]{0:T(128)}, f32[32]{0:T(128)}) custom-call(f32[16,1,128]{2,1,0:T(1,128)S(1)} %all_to_all.11.shares_ref, f32[1,128]{1,0:T(1,128)S(1)} %get-tuple-element.13.held_log_ref), custom_call_target="tpu_custom_call" | custom-call | tf_op jit(solution)/shard_map/pallas_call | solution.py:191
Async XLA Ops:
  13.7 1.9 %collective-permute-start = (f32[40,128]{1,0:T(8,128)S(1)}, f32[40,128]{1,0:T(8,128)S(1)}, u32[]{:S(2)}, u32[]{:S(2)}) collective-permute-start(f32[40,128]{1,0:T(8,128)S(1)} %shard_map.60.refs_0_), channel_id=1, source_target_pairs={{0,1},{1,0},{2,3},{3,2},{4,5},{5,4},{6,7},{7,6},{8,9},{9,8},{10,11... | collective-permute-start | bytes 61448 | tf_op jit(solution)/shard_map/ppermute | solution.py:185

commit v2 on v1

--- a/solution.py
+++ b/solution.py
@@ -61,29 +61,27 @@
     target_ref[...] = jnp.log(held_counts[...].astype(jnp.float32) / TABLE_ROWS + smoothing)
 
 
-def terms_kernel(width, blocks_ref, bounds_ref, spread_ref, out_ref):
-    dims, queries = bounds_ref.shape[1:]
-    count = blocks_ref.shape[0]
-    per_piece = 128 // width
-    group = min(count, 4 * per_piece)
-
+def limits(bounds_ref):
     low, high = bounds_ref[0], bounds_ref[1]
     limited = (high - low) != GRID
-    at = lax.broadcasted_iota(jnp.int32, (dims, queries), 0)
-    first = jnp.min(jnp.where(limited, at, dims), axis=0, keepdims=True)
+    at = lax.broadcasted_iota(jnp.int32, low.shape, 0)
+    first = jnp.min(jnp.where(limited, at, low.shape[0]), axis=0, keepdims=True)
     last = jnp.max(jnp.where(limited, at, -1), axis=0, keepdims=True)
-    chosen = [at == first, limited & (at > first) & (at < last), at == last]
-
+    return limited, [at == first, limited & (at > first) & (at < last), at == last]
+
+
+def select(masks, bounds_ref, spread_ref):
+    limited, chosen = masks
+    dims, queries = limited.shape
     row = lax.broadcasted_iota(jnp.int32, (dims, dims), 0)
     column = lax.broadcasted_iota(jnp.int32, (dims, dims), 1)
     spread = jnp.sum(jnp.where(row == column, spread_ref[...], 0.0), axis=1, keepdims=True)
     unit = ROOT_HALF / spread
 
     pick = lambda mask, values: jnp.sum(jnp.where(mask, values, 0.0), axis=0, keepdims=True)
-    low = low.astype(jnp.float32) * unit
-    high = high.astype(jnp.float32) * unit
-    low_at = [pick(mask, low) for mask in chosen]
-    high_at = [pick(mask, high) for mask in chosen]
+    low = bounds_ref[0].astype(jnp.float32) * unit
+    high = bounds_ref[1].astype(jnp.float32) * unit
+    ends = [pick(mask, low) for mask in chosen] + [pick(mask, high) for mask in chosen]
 
     ones = [mask.astype(jnp.float32).astype(jnp.bfloat16) for mask in chosen]
     free = jnp.where(limited, 0.0, 1.0).astype(jnp.bfloat16)
@@ -93,6 +91,16 @@
         + [jnp.concatenate([none] * LIMITED + [free], axis=1)] * 3,
         axis=0,
     )
+    return right, ends, unit
+
+
+def terms(width, blocks_ref, masks, right, ends, unit):
+    limited, chosen = masks
+    dims, queries = limited.shape
+    count = blocks_ref.shape[0]
+    per_piece = 128 // width
+    group = min(count, 4 * per_piece)
+    low_at, high_at = ends[:LIMITED], ends[LIMITED:]
 
     def step(picked, sums):
         others = jnp.exp2(picked[:, LIMITED * queries :])
@@ -153,22 +161,37 @@
     deriv = jnp.where(limited, 0.0, deriv * (SLOPE / 4))
     for mask, s in zip(chosen, sums[1:]):
         deriv = jnp.where(mask, s * (SLOPE / 4), deriv)
-    out_ref[:dims, :] = deriv
-    out_ref[dims:, :] = jnp.broadcast_to(sums[0] * 0.125, (8, queries))
-
-
-def finish_kernel(sample_total, query_total, *refs):
-    part_refs, (target_ref, log_ref, share_ref) = refs[:-3], refs[-3:]
-    whole = tree_sum([ref[...] for ref in part_refs])
-    dims, queries = whole.shape[0] - 8, whole.shape[1]
+    return jnp.concatenate([deriv, jnp.broadcast_to(sums[0] * 0.125, (8, queries))], axis=0)
+
+
+def own_kernel(width, blocks_ref, bounds_ref, spread_ref, part_ref, right_ref, ends_ref, unit_ref):
+    masks = limits(bounds_ref)
+    right, ends, unit = select(masks, bounds_ref, spread_ref)
+    part_ref[...] = terms(width, blocks_ref, masks, right, ends, unit)
+    right_ref[...] = right
+    for i, end in enumerate(ends):
+        ends_ref[i : i + 1, :] = end
+    unit_ref[...] = jnp.broadcast_to(unit, unit_ref.shape)
+
+
+def other_kernel(width, sample_total, query_total, *refs):
+    blocks_refs = refs[:-8]
+    part_ref, right_ref, ends_ref, unit_ref, bounds_ref, target_ref, log_ref, share_ref = refs[-8:]
+    masks = limits(bounds_ref)
+    right, unit = right_ref[...], unit_ref[:, :1]
+    ends = [ends_ref[i : i + 1, :] for i in range(2 * LIMITED)]
+    parts = [part_ref[...]]
+    parts += [terms(width, blocks_ref, masks, right, ends, unit) for blocks_ref in blocks_refs]
+    whole = tree_sum(parts)
+    dims, queries = masks[0].shape
     smoothing = 1.0 / TABLE_ROWS
     estimate = whole[dims : dims + 1] / sample_total
     log_est = jnp.log(estimate + smoothing)
     log_ref[...] = log_est
     weight = 2.0 * (log_est - target_ref[...]) / (query_total * (estimate + smoothing))
-    terms = whole[:dims] * (weight / sample_total)
-    terms = jnp.concatenate([terms, jnp.zeros((queries - dims, queries), jnp.float32)], axis=0)
-    share = jnp.sum(terms.T, axis=0, keepdims=True)
+    terms_at = whole[:dims] * (weight / sample_total)
+    terms_at = jnp.concatenate([terms_at, jnp.zeros((queries - dims, queries), jnp.float32)], axis=0)
+    share = jnp.sum(terms_at.T, axis=0, keepdims=True)
     for peer in range(share_ref.shape[0]):
         share_ref[peer] = share
 
@@ -186,7 +209,7 @@
     ]
 
 
-def call(kernel, args, outs, scratch=(), placed=pltpu.VMEM):
+def call(kernel, args, outs, scratch=(), placed=pltpu.VMEM, cost=None):
     single = len(outs) == 1
     return pl.pallas_call(
         kernel,
@@ -196,6 +219,7 @@
         if single
         else [pl.BlockSpec(memory_space=pltpu.VMEM)] * len(outs),
         scratch_shapes=list(scratch),
+        cost_estimate=cost,
         compiler_params=pltpu.CompilerParams(vmem_limit_bytes=32 << 20),
     )(*args)
 
@@ -234,14 +258,24 @@
     ]
     exchange = lambda x: lax.all_to_all(x, ("blk", "grp"), 0, 0, axis_index_groups=groups)
     gathered = exchange(packed)
-    part = call(
-        functools.partial(terms_kernel, width),
+    others = everyone(gathered, "grp")[1:]
+    elements = LIMITED * gathered.shape[0] * width * queries
+    part, right, ends, unit = call(
+        functools.partial(own_kernel, width),
         [gathered, bounds, spread],
-        [shape(dims + 8, queries)],
+        [
+            shape(dims + 8, queries),
+            jax.ShapeDtypeStruct((6 * dims, (LIMITED + 1) * queries), jnp.bfloat16),
+            shape(8, queries),
+            shape(dims, queries),
+        ],
+        cost=pl.CostEstimate(
+            flops=100 * elements, bytes_accessed=64 * elements, transcendentals=4 * elements
+        ),
     )
     log_est, share = call(
-        functools.partial(finish_kernel, sample_total, query_total),
-        everyone(part, "grp") + [target],
+        functools.partial(other_kernel, width, sample_total, query_total),
+        others + [part, right, ends, unit, bounds, target],
         [shape(1, queries), shape(blocks, 1, queries)],
     )
     shares = exchange(share)

time: 25.6 us -> 25.7 us (level)
  Pallas kernels: 2.49 us -> 3.61 us
  waiting for transfers between devices: 0.84 us -> 0.01 us
    pallas_call x4, Pallas kernels: 2.49 us -> 3.61 us  [call(): pl.pallas_call(kernel, out_shape=outs[0] if single else outs, in_specs=[p...]
    ppermute x1, waiting for transfers between devices: 0.84 us -> 0.01 us  [everyone(): lax.ppermute(x, axis, [(i, i ^ offset) for i in range(size)])]
  transfers between devices with their start and end apart: 1 -> 1, of which waited for: 1 -> 0; matrix products, arithmetic and copies ran while one was open for 0% -> 0% of each run, Pallas kernels for 0% -> 4%
where the time goes in v2:
time: 25.7 us; the launch traced here: 25.3 us
  blocking collectives  20.1 us (78%)
  Pallas kernels  3.61 us (14%)
  starting transfers between devices  0.95 us (4%)
  between operations  0.66 us (3%)
    all_to_all x2, blocking collectives, on_device(): lax.all_to_all(x, ('blk', 'grp'), 0, 0, axis_index_groups=groups)  20.1 us
    pallas_call x4, Pallas kernels, call(): pl.pallas_call(kernel, out_shape=outs[0] if single else outs, in_specs=[p...  3.61 us
    ppermute x1, starting transfers between devices, everyone(): lax.ppermute(x, axis, [(i, i ^ offset) for i in range(size)])  0.95 us
  transfers between devices with their start and end apart: 1, of which 0 were waited for; matrix products, arithmetic and copies ran while one was open for 0% of the time, Pallas kernels for 4%

profile of v2, /device:TPU:0, one launch (start us, length us, event | category | flops | bytes accessed | tf_op | source)
XLA Modules:
  0.0 25.3 jit_solution(13512540696326474052)
XLA Ops:
  0.6 0.8 %shard_map.59 = (f32[16,8,128]{2,1,0:T(8,128)S(1)}, s32[2,32,128]{2,1,0:T(8,128)S(1)}, f32[1,32]{1,0:T(1,128)S(1)}, f32[1,128]{1,0:T(1,128)S(1)}) custom-call(f32[32,32]{1,0:T(8,128)} %x_ref.1, s32[2,32,128]{2,1,0:T(8,128)} %bounds_ref.1, f32[1,32]{1,0:T(1,128)} %bitcast.2, s32[1,128]{1,0:T(1,128)} %bitcast.3), custom_call_target="tpu_custom_call" | custom-call | tf_op jit(solution)/shard_map/pallas_call | solution.py:214
  1.5 11.2 %all_to_all.10.blocks_ref = f32[16,8,128]{2,1,0:T(8,128)S(1)} all-to-all(f32[16,8,128]{2,1,0:T(8,128)S(1)} %get-tuple-element.12), channel_id=1, replica_groups={{30,28,26,24,22,20,18,16,14,12,10,8,6,4,2,1},{31,29,27,25,23,21,19,17,1..., dimensions={0} | all-to-all | bytes 131072 | tf_op jit(solution)/shard_map/all_to_all | solution.py:259
  12.7 0.9 %collective-permute-start = (f32[16,8,128]{2,1,0:T(8,128)S(1)}, f32[16,8,128]{2,1,0:T(8,128)S(1)}, u32[]{:S(2)}, u32[]{:S(2)}) collective-permute-start(f32[16,8,128]{2,1,0:T(8,128)S(1)} %all_to_all.10.blocks_ref), channel_id=1, source_target_pairs={{0,1},{1,0},{2,3},{3,2},{4,5},{5,4},{6,7},{7,6},{8,9},{9,8},{10,11... | collective-permute-start | bytes 196616 | tf_op jit(solution)/shard_map/ppermute | solution.py:208
  13.6 1.0 %shard_map.60 = (f32[40,128]{1,0:T(8,128)S(1)}, bf16[192,512]{1,0:T(8,128)(2,1)S(1)}, f32[8,128]{1,0:T(8,128)S(1)}, f32[32,128]{1,0:T(8,128)S(1)}) custom-call(f32[16,8,128]{2,1,0:T(8,128)S(1)} %all_to_all.10.blocks_ref, s32[2,32,128]{2,1,0:T(8,128)S(1)} %get-tuple-element.13.bounds_ref.refs_5_, f32[1,32]{1,0:T(1,128)S(1)} %get-tuple-element.14.spread_ref), custom_call_target="tpu_custom_call" | custom-call | flops 19660800 | bytes 12582912 | tf_op jit(solution)/shard_map/pallas_call | solution.py:214
  14.7 0.0 collective-permute-done.refs_0_
  14.7 1.2 %shard_map.61 = (f32[1,128]{1,0:T(1,128)S(1)}, f32[16,1,128]{2,1,0:T(1,128)S(1)}) custom-call(f32[16,8,128]{2,1,0:T(8,128)S(1)} %collective-permute-done.refs_0_, f32[40,128]{1,0:T(8,128)S(1)} %get-tuple-element.15.refs_1_, bf16[192,512]{1,0:T(8,128)(2,1)S(1)} %get-tuple-element.16.refs_2_, f32[8,128]{1,0:T(8,128)S(1)} %get-tuple-element.17.refs_3_, ...), custom_call_target="tpu_custom_call" | custom-call | tf_op jit(solution)/shard_map/pallas_call | solution.py:214
  15.9 8.9 %all_to_all.11.shares_ref = f32[16,1,128]{2,1,0:T(1,128)S(1)} all-to-all(f32[16,1,128]{2,1,0:T(1,128)S(1)} %get-tuple-element.20), channel_id=1, replica_groups={{30,28,26,24,22,20,18,16,14,12,10,8,6,4,2,1},{31,29,27,25,23,21,19,17,1..., dimensions={0} | all-to-all | bytes 16384 | tf_op jit(solution)/shard_map/all_to_all | solution.py:259
  24.8 0.5 %shard_map.62 = (f32[128]{0:T(128)}, f32[32]{0:T(128)}) custom-call(f32[16,1,128]{2,1,0:T(1,128)S(1)} %all_to_all.11.shares_ref, f32[1,128]{1,0:T(1,128)S(1)} %get-tuple-element.21.held_log_ref), custom_call_target="tpu_custom_call" | custom-call | tf_op jit(solution)/shard_map/pallas_call | solution.py:214
Async XLA Ops:
  12.7 2.0 %collective-permute-start = (f32[16,8,128]{2,1,0:T(8,128)S(1)}, f32[16,8,128]{2,1,0:T(8,128)S(1)}, u32[]{:S(2)}, u32[]{:S(2)}) collective-permute-start(f32[16,8,128]{2,1,0:T(8,128)S(1)} %all_to_all.10.blocks_ref), channel_id=1, source_target_pairs={{0,1},{1,0},{2,3},{3,2},{4,5},{5,4},{6,7},{7,6},{8,9},{9,8},{10,11... | collective-permute-start | bytes 196616 | tf_op jit(solution)/shard_map/ppermute | solution.py:208

commit v3 on v0

--- a/solution.py
+++ b/solution.py
@@ -227,8 +227,15 @@
         [pltpu.VMEM((dims, width), jnp.float32), counts_vector, pltpu.SemaphoreType.DMA((4,))],
         placed=pl.ANY,
     )
-    order = [list(reversed(range(blocks)))]
-    gathered = lax.all_to_all(packed, "blk", 0, 0, axis_index_groups=order)
+    def exchange(x, turned, lasts):
+        groups = []
+        for c in range(copies):
+            blocks_of = [b for b in reversed(range(blocks)) if b != lasts[c]] + [lasts[c]]
+            groups.append([b * copies + (c + (b == turned)) % copies for b in blocks_of])
+        return lax.all_to_all(x, ("blk", "grp"), 0, 0, axis_index_groups=groups)
+
+    middle = blocks // 3
+    gathered = exchange(packed, middle, [middle] * (copies - 1) + [middle + 1])
     part = call(
         functools.partial(terms_kernel, width),
         [gathered, bounds, spread],
@@ -239,7 +246,7 @@
         everyone(part, "grp") + [target],
         [shape(1, queries), shape(blocks, 1, queries)],
     )
-    shares = lax.all_to_all(share, "blk", 0, 0, axis_index_groups=order)
+    shares = exchange(share, 0, [0] * copies)
     return call(last_kernel, [shares, log_est], [shape(queries), shape(dims)])
 
 

time: 26.5 us -> 26.2 us (0.989)
  blocking collectives: 21.8 us -> 21.3 us
    all_to_all x2, blocking collectives: 21.8 us -> 21.3 us  [exchange(): return lax.all_to_all(x, ('blk', 'grp'), 0, 0, axis_index_groups=groups)]
where the time goes in v3:
time: 26.2 us; the launch traced here: 25.7 us
  blocking collectives  21.3 us (81%)
  Pallas kernels  2.49 us (10%)
  waiting for transfers between devices  1.18 us (5%)
  between operations  0.66 us (3%)
    all_to_all x2, blocking collectives, exchange(): return lax.all_to_all(x, ('blk', 'grp'), 0, 0, axis_index_groups=groups)  21.3 us
    pallas_call x4, Pallas kernels, call(): pl.pallas_call(kernel, out_shape=outs[0] if single else outs, in_specs=[p...  2.49 us
    ppermute x1, waiting for transfers between devices, everyone(): lax.ppermute(x, axis, [(i, i ^ offset) for i in range(size)])  1.18 us
  transfers between devices with their start and end apart: 1, of which 1 were waited for; matrix products, arithmetic and copies ran while one was open for 0% of the time, Pallas kernels for 0%

profile of v3, /device:TPU:0, one launch (start us, length us, event | category | flops | bytes accessed | tf_op | source)
XLA Modules:
  0.0 25.7 jit_solution(5046096485783136826)
XLA Ops:
  0.6 0.8 %shard_map.59 = (f32[16,8,128]{2,1,0:T(8,128)S(1)}, s32[2,32,128]{2,1,0:T(8,128)S(1)}, f32[1,32]{1,0:T(1,128)S(1)}, f32[1,128]{1,0:T(1,128)S(1)}) custom-call(f32[32,32]{1,0:T(8,128)} %x_ref.1, s32[2,32,128]{2,1,0:T(8,128)} %bounds_ref.1, f32[1,32]{1,0:T(1,128)} %bitcast.2, s32[1,128]{1,0:T(1,128)} %bitcast.3), custom_call_target="tpu_custom_call" | custom-call | tf_op jit(solution)/shard_map/pallas_call | solution.py:191
  1.5 12.4 %all_to_all.10.blocks_ref = f32[16,8,128]{2,1,0:T(8,128)S(1)} all-to-all(f32[16,8,128]{2,1,0:T(8,128)S(1)} %get-tuple-element.8), channel_id=1, replica_groups={{30,28,26,24,22,20,18,16,14,12,8,6,4,2,0,11},{31,29,27,25,23,21,19,17,1..., dimensions={0} | all-to-all | bytes 131072 | tf_op jit(solution)/shard_map/all_to_all | solution.py:235
  13.8 1.0 %shard_map.60.refs_0_ = f32[40,128]{1,0:T(8,128)S(1)} custom-call(f32[16,8,128]{2,1,0:T(8,128)S(1)} %all_to_all.10.blocks_ref, s32[2,32,128]{2,1,0:T(8,128)S(1)} %get-tuple-element.9.bounds_ref, f32[1,32]{1,0:T(1,128)S(1)} %get-tuple-element.10.spread_ref), custom_call_target="tpu_custom_call" | custom-call | tf_op jit(solution)/shard_map/pallas_call | solution.py:191
  14.9 0.1 collective-permute-start
  14.9 1.2 %collective-permute-done.refs_1_ = f32[40,128]{1,0:T(8,128)S(1)} collective-permute-done((f32[40,128]{1,0:T(8,128)S(1)}, f32[40,128]{1,0:T(8,128)S(1)}, u32[]{:S(2)}, u32[]{:S(2)}) %collective-permute-start) | collective-permute-done | bytes 20512 | tf_op jit(solution)/shard_map/ppermute | solution.py:185
  16.1 0.1 shard_map.61
  16.2 8.9 %all_to_all.11.shares_ref = f32[16,1,128]{2,1,0:T(1,128)S(1)} all-to-all(f32[16,1,128]{2,1,0:T(1,128)S(1)} %get-tuple-element.12), channel_id=1, replica_groups={{30,28,26,24,22,20,18,16,14,12,10,8,6,4,2,1},{31,29,27,25,23,21,19,17,1..., dimensions={0} | all-to-all | bytes 16384 | tf_op jit(solution)/shard_map/all_to_all | solution.py:235
  25.2 0.5 %shard_map.62 = (f32[128]{0:T(128)}, f32[32]{0:T(128)}) custom-call(f32[16,1,128]{2,1,0:T(1,128)S(1)} %all_to_all.11.shares_ref, f32[1,128]{1,0:T(1,128)S(1)} %get-tuple-element.13.held_log_ref), custom_call_target="tpu_custom_call" | custom-call | tf_op jit(solution)/shard_map/pallas_call | solution.py:191
Async XLA Ops:
  14.9 1.3 %collective-permute-start = (f32[40,128]{1,0:T(8,128)S(1)}, f32[40,128]{1,0:T(8,128)S(1)}, u32[]{:S(2)}, u32[]{:S(2)}) collective-permute-start(f32[40,128]{1,0:T(8,128)S(1)} %shard_map.60.refs_0_), channel_id=1, source_target_pairs={{0,1},{1,0},{2,3},{3,2},{4,5},{5,4},{6,7},{7,6},{8,9},{9,8},{10,11... | collective-permute-start | bytes 61448 | tf_op jit(solution)/shard_map/ppermute | solution.py:185

commit v4 on v1

--- a/solution.py
+++ b/solution.py
@@ -51,8 +51,9 @@
     for copy in copies:
         copy.start()
     copies[0].wait()
-    rows = held_x.shape[0]
-    packed = jnp.concatenate([held_x[8 * j : 8 * (j + 1), :] for j in range(rows // 8)], axis=1)
+    rows = held_x.shape[1]
+    turned = held_x[...].T
+    packed = jnp.concatenate([turned[8 * j : 8 * (j + 1), :] for j in range(rows // 8)], axis=1)
     for peer in range(out_ref.shape[0]):
         out_ref[peer] = packed
     for copy in copies[1:]:
@@ -61,11 +62,11 @@
     target_ref[...] = jnp.log(held_counts[...].astype(jnp.float32) / TABLE_ROWS + smoothing)
 
 
-def terms_kernel(width, blocks_ref, bounds_ref, spread_ref, out_ref):
+def terms_kernel(blocks_ref, bounds_ref, spread_ref, out_ref):
     dims, queries = bounds_ref.shape[1:]
-    count = blocks_ref.shape[0]
-    per_piece = 128 // width
-    group = min(count, 4 * per_piece)
+    lanes = blocks_ref.shape[2]
+    pieces = lanes // dims
+    group = 128 // blocks_ref.shape[1]
 
     low, high = bounds_ref[0], bounds_ref[1]
     limited = (high - low) != GRID
@@ -74,10 +75,11 @@
     last = jnp.max(jnp.where(limited, at, -1), axis=0, keepdims=True)
     chosen = [at == first, limited & (at > first) & (at < last), at == last]
 
+    unit_row = ROOT_HALF / spread_ref[...]
     row = lax.broadcasted_iota(jnp.int32, (dims, dims), 0)
     column = lax.broadcasted_iota(jnp.int32, (dims, dims), 1)
-    spread = jnp.sum(jnp.where(row == column, spread_ref[...], 0.0), axis=1, keepdims=True)
-    unit = ROOT_HALF / spread
+    unit = jnp.sum(jnp.where(row == column, unit_row, 0.0), axis=1, keepdims=True)
+    unit_row = jnp.concatenate([unit_row] * pieces, axis=1)
 
     pick = lambda mask, values: jnp.sum(jnp.where(mask, values, 0.0), axis=0, keepdims=True)
     low = low.astype(jnp.float32) * unit
@@ -85,20 +87,16 @@
     low_at = [pick(mask, low) for mask in chosen]
     high_at = [pick(mask, high) for mask in chosen]
 
-    ones = [mask.astype(jnp.float32).astype(jnp.bfloat16) for mask in chosen]
-    free = jnp.where(limited, 0.0, 1.0).astype(jnp.bfloat16)
-    none = jnp.zeros_like(free)
-    right = jnp.concatenate(
-        [jnp.concatenate(ones + [none], axis=1)] * 3
-        + [jnp.concatenate([none] * LIMITED + [free], axis=1)] * 3,
-        axis=0,
-    )
-
-    def step(picked, sums):
-        others = jnp.exp2(picked[:, LIMITED * queries :])
+    as_ones = lambda mask: jnp.where(mask, 1.0, 0.0).astype(jnp.bfloat16)
+    one_hot = jnp.concatenate([as_ones(mask) for mask in chosen], axis=1)
+    one_hot = jnp.concatenate([one_hot] * pieces, axis=0)
+    free = jnp.concatenate([as_ones(jnp.logical_not(limited))] * pieces, axis=0)
+
+    def step(boxes, others, sums):
+        others = jnp.exp2(others)
         mass, slope = [], []
         for k in range(LIMITED):
-            points = picked[:, k * queries : (k + 1) * queries]
+            points = boxes[:, k * queries : (k + 1) * queries]
             m, s = box_terms(low_at[k] - points, high_at[k] - points)
             mass.append(m)
             slope.append(s)
@@ -112,41 +110,44 @@
             sums[3] + last_two * slope[2],
         )
 
-    def piece(start, totals):
+    place = lax.broadcasted_iota(jnp.int32, (1, lanes), 1) // dims
+
+    def thirds(x):
+        head = x.astype(jnp.bfloat16).astype(jnp.float32)
+        rest = x - head
+        tail = rest - rest.astype(jnp.bfloat16).astype(jnp.float32)
+        return [x, pltpu.roll(rest, dims, 1), pltpu.roll(tail, 2 * dims, 1)]
+
+    def left(parts, j):
+        x = jnp.zeros_like(parts[0])
+        for p, part in enumerate(parts):
+            x = jnp.where(place == (j + p) % pieces, part, x)
+        return x.astype(jnp.bfloat16)
+
+    def chunk(number, totals):
         sums, products = totals[:-1], totals[-1]
-        some = [blocks_ref[start + b] for b in range(per_piece)]
-        x = unit * jnp.concatenate(
-            [
-                jnp.concatenate([block[:, width * j : width * (j + 1)] for block in some], axis=1)
-                for j in range(dims // 8)
-            ],
-            axis=0,
-        )
-        full, slope = box_terms(-x, float(GRID) * unit - x)
-        ratio = jnp.concatenate(split(slope / full, 2), axis=0)
-        left = jnp.concatenate(split(x, 3) + split(jnp.log(0.5 * full) * LOG2_E, 3), axis=0)
-        picked = lax.dot_general(
-            left, right, (((0,), (0,)), ((), ())), preferred_element_type=jnp.float32
-        )
-        inside = []
-        for at_row in range(0, per_piece * width, 16):
-            whole, sums = step(picked[at_row : at_row + 16], sums)
-            inside.append(jnp.concatenate(split(whole, 2), axis=1))
-        inside = jnp.concatenate(inside, axis=0)
-        products = products + jnp.dot(ratio, inside, preferred_element_type=jnp.float32)
+        x = blocks_ref[pl.ds(number * group, group)].reshape(128, lanes) * unit_row
+        points = thirds(x)
+        full, slope = box_terms(-x, float(GRID) * unit_row - x)
+        logs = thirds(jnp.log(0.5 * full) * LOG2_E)
+        ratio = split((slope / full).T, 2)
+        for j in range(pieces):
+            boxes = jnp.dot(left(points, j), one_hot, preferred_element_type=jnp.float32)
+            others = jnp.dot(left(logs, j), free, preferred_element_type=jnp.float32)
+            inside = []
+            for r in range(0, 128, 16):
+                whole, sums = step(boxes[r : r + 16], others[r : r + 16], sums)
+                inside.append(jnp.concatenate(split(whole, 2), axis=1))
+            ratio_at = jnp.concatenate([part[j * dims : (j + 1) * dims] for part in ratio], axis=0)
+            products = products + jnp.dot(
+                ratio_at, jnp.concatenate(inside, axis=0), preferred_element_type=jnp.float32
+            )
         return (*sums, products)
-
-    def pieces(number, totals):
-        for start in range(0, group, per_piece):
-            totals = piece(number * group + start, totals)
-        return totals
 
     zero = jnp.zeros((16, queries), jnp.float32)
     totals = (zero,) * (1 + LIMITED) + (jnp.zeros((2 * dims, 2 * queries), jnp.float32),)
-    if count == group:
-        totals = pieces(0, totals)
-    else:
-        totals = lax.fori_loop(0, count // group, pieces, totals)
+    chunks = blocks_ref.shape[0] // group
+    totals = chunk(0, totals) if chunks == 1 else lax.fori_loop(0, chunks, chunk, totals)
     sums = [jnp.sum(s, axis=0, keepdims=True) for s in totals[:-1]]
     products = totals[-1]
     deriv = products[:dims, :queries] + (products[dims:, :queries] + products[:dims, queries:])
@@ -235,7 +236,7 @@
     exchange = lambda x: lax.all_to_all(x, ("blk", "grp"), 0, 0, axis_index_groups=groups)
     gathered = exchange(packed)
     part = call(
-        functools.partial(terms_kernel, width),
+        terms_kernel,
         [gathered, bounds, spread],
         [shape(dims + 8, queries)],
     )

time: 25.6 us -> 25.8 us (level)
  no operation moved by 1% of the time
where the time goes in v4:
time: 25.8 us; the launch traced here: 25.3 us
  blocking collectives  20.1 us (78%)
  Pallas kernels  2.73 us (11%)
  starting transfers between devices  1.01 us (4%)
  waiting for transfers between devices  0.84 us (3%)
  between operations  0.66 us (3%)
    all_to_all x2, blocking collectives, on_device(): lax.all_to_all(x, ('blk', 'grp'), 0, 0, axis_index_groups=groups)  20.1 us
    pallas_call x4, Pallas kernels, call(): pl.pallas_call(kernel, out_shape=outs[0] if single else outs, in_specs=[p...  2.73 us
    ppermute x1, starting transfers between devices, everyone(): lax.ppermute(x, axis, [(i, i ^ offset) for i in range(size)])  1.01 us
    ppermute x1, waiting for transfers between devices, everyone(): lax.ppermute(x, axis, [(i, i ^ offset) for i in range(size)])  0.84 us
  transfers between devices with their start and end apart: 1, of which 1 were waited for; matrix products, arithmetic and copies ran while one was open for 0% of the time, Pallas kernels for 0%

profile of v4, /device:TPU:0, one launch (start us, length us, event | category | flops | bytes accessed | tf_op | source)
XLA Modules:
  0.0 25.3 jit_solution(16713604299510291395)
XLA Ops:
  0.6 0.9 %shard_map.59 = (f32[16,8,128]{2,1,0:T(8,128)S(1)}, s32[2,32,128]{2,1,0:T(8,128)S(1)}, f32[1,32]{1,0:T(1,128)S(1)}, f32[1,128]{1,0:T(1,128)S(1)}) custom-call(f32[32,32]{1,0:T(8,128)} %x_ref.1, s32[2,32,128]{2,1,0:T(8,128)} %bounds_ref.1, f32[1,32]{1,0:T(1,128)} %bitcast.2, s32[1,128]{1,0:T(1,128)} %bitcast.3), custom_call_target="tpu_custom_call" | custom-call | tf_op jit(solution)/shard_map/pallas_call | solution.py:192
  1.6 11.2 %all_to_all.10.blocks_ref = f32[16,8,128]{2,1,0:T(8,128)S(1)} all-to-all(f32[16,8,128]{2,1,0:T(8,128)S(1)} %get-tuple-element.8), channel_id=1, replica_groups={{30,28,26,24,22,20,18,16,14,12,10,8,6,4,2,1},{31,29,27,25,23,21,19,17,1..., dimensions={0} | all-to-all | bytes 131072 | tf_op jit(solution)/shard_map/all_to_all | solution.py:236
  12.8 1.2 %shard_map.60.refs_0_ = f32[40,128]{1,0:T(8,128)S(1)} custom-call(f32[16,8,128]{2,1,0:T(8,128)S(1)} %all_to_all.10.blocks_ref, s32[2,32,128]{2,1,0:T(8,128)S(1)} %get-tuple-element.9.bounds_ref, f32[1,32]{1,0:T(1,128)S(1)} %get-tuple-element.10.spread_ref), custom_call_target="tpu_custom_call" | custom-call | tf_op jit(solution)/shard_map/pallas_call | solution.py:192
  13.9 1.0 %collective-permute-start = (f32[40,128]{1,0:T(8,128)S(1)}, f32[40,128]{1,0:T(8,128)S(1)}, u32[]{:S(2)}, u32[]{:S(2)}) collective-permute-start(f32[40,128]{1,0:T(8,128)S(1)} %shard_map.60.refs_0_), channel_id=1, source_target_pairs={{0,1},{1,0},{2,3},{3,2},{4,5},{5,4},{6,7},{7,6},{8,9},{9,8},{10,11... | collective-permute-start | bytes 61448 | tf_op jit(solution)/shard_map/ppermute | solution.py:186
  15.0 0.8 %collective-permute-done.refs_1_ = f32[40,128]{1,0:T(8,128)S(1)} collective-permute-done((f32[40,128]{1,0:T(8,128)S(1)}, f32[40,128]{1,0:T(8,128)S(1)}, u32[]{:S(2)}, u32[]{:S(2)}) %collective-permute-start) | collective-permute-done | bytes 20512 | tf_op jit(solution)/shard_map/ppermute | solution.py:186
  15.8 0.1 shard_map.61
  15.9 8.9 %all_to_all.11.shares_ref = f32[16,1,128]{2,1,0:T(1,128)S(1)} all-to-all(f32[16,1,128]{2,1,0:T(1,128)S(1)} %get-tuple-element.12), channel_id=1, replica_groups={{30,28,26,24,22,20,18,16,14,12,10,8,6,4,2,1},{31,29,27,25,23,21,19,17,1..., dimensions={0} | all-to-all | bytes 16384 | tf_op jit(solution)/shard_map/all_to_all | solution.py:236
  24.8 0.5 %shard_map.62 = (f32[128]{0:T(128)}, f32[32]{0:T(128)}) custom-call(f32[16,1,128]{2,1,0:T(1,128)S(1)} %all_to_all.11.shares_ref, f32[1,128]{1,0:T(1,128)S(1)} %get-tuple-element.13.held_log_ref), custom_call_target="tpu_custom_call" | custom-call | tf_op jit(solution)/shard_map/pallas_call | solution.py:192
Async XLA Ops:
  13.9 1.9 %collective-permute-start = (f32[40,128]{1,0:T(8,128)S(1)}, f32[40,128]{1,0:T(8,128)S(1)}, u32[]{:S(2)}, u32[]{:S(2)}) collective-permute-start(f32[40,128]{1,0:T(8,128)S(1)} %shard_map.60.refs_0_), channel_id=1, source_target_pairs={{0,1},{1,0},{2,3},{3,2},{4,5},{5,4},{6,7},{7,6},{8,9},{9,8},{10,11... | collective-permute-start | bytes 61448 | tf_op jit(solution)/shard_map/ppermute | solution.py:186

commit v5 on v1

--- a/solution.py
+++ b/solution.py
@@ -64,8 +64,7 @@
 def terms_kernel(width, blocks_ref, bounds_ref, spread_ref, out_ref):
     dims, queries = bounds_ref.shape[1:]
     count = blocks_ref.shape[0]
-    per_piece = 128 // width
-    group = min(count, 4 * per_piece)
+    group = min(count, 512 // width)
 
     low, high = bounds_ref[0], bounds_ref[1]
     limited = (high - low) != GRID
@@ -112,9 +111,9 @@
             sums[3] + last_two * slope[2],
         )
 
-    def piece(start, totals):
+    def chunk(number, totals):
         sums, products = totals[:-1], totals[-1]
-        some = [blocks_ref[start + b] for b in range(per_piece)]
+        some = [blocks_ref[number * group + b] for b in range(group)]
         x = unit * jnp.concatenate(
             [
                 jnp.concatenate([block[:, width * j : width * (j + 1)] for block in some], axis=1)
@@ -128,25 +127,25 @@
         picked = lax.dot_general(
             left, right, (((0,), (0,)), ((), ())), preferred_element_type=jnp.float32
         )
-        inside = []
-        for at_row in range(0, per_piece * width, 16):
-            whole, sums = step(picked[at_row : at_row + 16], sums)
-            inside.append(jnp.concatenate(split(whole, 2), axis=1))
-        inside = jnp.concatenate(inside, axis=0)
-        products = products + jnp.dot(ratio, inside, preferred_element_type=jnp.float32)
+        samples = group * width
+        for start in range(0, samples, 256):
+            inside = []
+            for at_row in range(start, start + 256, 16):
+                whole, sums = step(picked[at_row : at_row + 16], sums)
+                inside.append(jnp.concatenate(split(whole, 2), axis=1))
+            products = products + jnp.dot(
+                ratio[:, start : start + 256],
+                jnp.concatenate(inside, axis=0),
+                preferred_element_type=jnp.float32,
+            )
         return (*sums, products)
-
-    def pieces(number, totals):
-        for start in range(0, group, per_piece):
-            totals = piece(number * group + start, totals)
-        return totals
 
     zero = jnp.zeros((16, queries), jnp.float32)
     totals = (zero,) * (1 + LIMITED) + (jnp.zeros((2 * dims, 2 * queries), jnp.float32),)
     if count == group:
-        totals = pieces(0, totals)
+        totals = chunk(0, totals)
     else:
-        totals = lax.fori_loop(0, count // group, pieces, totals)
+        totals = lax.fori_loop(0, count // group, chunk, totals)
     sums = [jnp.sum(s, axis=0, keepdims=True) for s in totals[:-1]]
     products = totals[-1]
     deriv = products[:dims, :queries] + (products[dims:, :queries] + products[:dims, queries:])

time: 25.6 us -> 25.6 us (level)
  no operation moved by 1% of the time
where the time goes in v5:
time: 25.6 us; the launch traced here: 25.1 us
  blocking collectives  20.1 us (79%)
  Pallas kernels  2.49 us (10%)
  starting transfers between devices  1.01 us (4%)
  waiting for transfers between devices  0.84 us (3%)
  between operations  0.66 us (3%)
    all_to_all x2, blocking collectives, on_device(): lax.all_to_all(x, ('blk', 'grp'), 0, 0, axis_index_groups=groups)  20.1 us
    pallas_call x4, Pallas kernels, call(): pl.pallas_call(kernel, out_shape=outs[0] if single else outs, in_specs=[p...  2.49 us
    ppermute x1, starting transfers between devices, everyone(): lax.ppermute(x, axis, [(i, i ^ offset) for i in range(size)])  1.01 us
    ppermute x1, waiting for transfers between devices, everyone(): lax.ppermute(x, axis, [(i, i ^ offset) for i in range(size)])  0.84 us
  transfers between devices with their start and end apart: 1, of which 1 were waited for; matrix products, arithmetic and copies ran while one was open for 0% of the time, Pallas kernels for 0%

profile of v5, /device:TPU:0, one launch (start us, length us, event | category | flops | bytes accessed | tf_op | source)
XLA Modules:
  0.0 25.1 jit_solution(9087122650945784831)
XLA Ops:
  0.6 0.8 %shard_map.59 = (f32[16,8,128]{2,1,0:T(8,128)S(1)}, s32[2,32,128]{2,1,0:T(8,128)S(1)}, f32[1,32]{1,0:T(1,128)S(1)}, f32[1,128]{1,0:T(1,128)S(1)}) custom-call(f32[32,32]{1,0:T(8,128)} %x_ref.1, s32[2,32,128]{2,1,0:T(8,128)} %bounds_ref.1, f32[1,32]{1,0:T(1,128)} %bitcast.2, s32[1,128]{1,0:T(1,128)} %bitcast.3), custom_call_target="tpu_custom_call" | custom-call | tf_op jit(solution)/shard_map/pallas_call | solution.py:190
  1.5 11.2 %all_to_all.10.blocks_ref = f32[16,8,128]{2,1,0:T(8,128)S(1)} all-to-all(f32[16,8,128]{2,1,0:T(8,128)S(1)} %get-tuple-element.8), channel_id=1, replica_groups={{30,28,26,24,22,20,18,16,14,12,10,8,6,4,2,1},{31,29,27,25,23,21,19,17,1..., dimensions={0} | all-to-all | bytes 131072 | tf_op jit(solution)/shard_map/all_to_all | solution.py:234
  12.7 1.0 %shard_map.60.refs_0_ = f32[40,128]{1,0:T(8,128)S(1)} custom-call(f32[16,8,128]{2,1,0:T(8,128)S(1)} %all_to_all.10.blocks_ref, s32[2,32,128]{2,1,0:T(8,128)S(1)} %get-tuple-element.9.bounds_ref, f32[1,32]{1,0:T(1,128)S(1)} %get-tuple-element.10.spread_ref), custom_call_target="tpu_custom_call" | custom-call | tf_op jit(solution)/shard_map/pallas_call | solution.py:190
  13.7 1.0 %collective-permute-start = (f32[40,128]{1,0:T(8,128)S(1)}, f32[40,128]{1,0:T(8,128)S(1)}, u32[]{:S(2)}, u32[]{:S(2)}) collective-permute-start(f32[40,128]{1,0:T(8,128)S(1)} %shard_map.60.refs_0_), channel_id=1, source_target_pairs={{0,1},{1,0},{2,3},{3,2},{4,5},{5,4},{6,7},{7,6},{8,9},{9,8},{10,11... | collective-permute-start | bytes 61448 | tf_op jit(solution)/shard_map/ppermute | solution.py:184
  14.7 0.8 %collective-permute-done.refs_1_ = f32[40,128]{1,0:T(8,128)S(1)} collective-permute-done((f32[40,128]{1,0:T(8,128)S(1)}, f32[40,128]{1,0:T(8,128)S(1)}, u32[]{:S(2)}, u32[]{:S(2)}) %collective-permute-start) | collective-permute-done | bytes 20512 | tf_op jit(solution)/shard_map/ppermute | solution.py:184
  15.6 0.1 shard_map.61
  15.7 8.9 %all_to_all.11.shares_ref = f32[16,1,128]{2,1,0:T(1,128)S(1)} all-to-all(f32[16,1,128]{2,1,0:T(1,128)S(1)} %get-tuple-element.12), channel_id=1, replica_groups={{30,28,26,24,22,20,18,16,14,12,10,8,6,4,2,1},{31,29,27,25,23,21,19,17,1..., dimensions={0} | all-to-all | bytes 16384 | tf_op jit(solution)/shard_map/all_to_all | solution.py:234
  24.6 0.5 %shard_map.62 = (f32[128]{0:T(128)}, f32[32]{0:T(128)}) custom-call(f32[16,1,128]{2,1,0:T(1,128)S(1)} %all_to_all.11.shares_ref, f32[1,128]{1,0:T(1,128)S(1)} %get-tuple-element.13.held_log_ref), custom_call_target="tpu_custom_call" | custom-call | tf_op jit(solution)/shard_map/pallas_call | solution.py:190
Async XLA Ops:
  13.7 1.9 %collective-permute-start = (f32[40,128]{1,0:T(8,128)S(1)}, f32[40,128]{1,0:T(8,128)S(1)}, u32[]{:S(2)}, u32[]{:S(2)}) collective-permute-start(f32[40,128]{1,0:T(8,128)S(1)} %shard_map.60.refs_0_), channel_id=1, source_target_pairs={{0,1},{1,0},{2,3},{3,2},{4,5},{5,4},{6,7},{7,6},{8,9},{9,8},{10,11... | collective-permute-start | bytes 61448 | tf_op jit(solution)/shard_map/ppermute | solution.py:184

commit v6 on v1

--- a/solution.py
+++ b/solution.py
@@ -82,34 +82,37 @@
     pick = lambda mask, values: jnp.sum(jnp.where(mask, values, 0.0), axis=0, keepdims=True)
     low = low.astype(jnp.float32) * unit
     high = high.astype(jnp.float32) * unit
-    low_at = [pick(mask, low) for mask in chosen]
-    high_at = [pick(mask, high) for mask in chosen]
-
-    ones = [mask.astype(jnp.float32).astype(jnp.bfloat16) for mask in chosen]
-    free = jnp.where(limited, 0.0, 1.0).astype(jnp.bfloat16)
-    none = jnp.zeros_like(free)
+    ends = [pick(mask, low) for mask in chosen] + [pick(mask, high) for mask in chosen]
+
+    minus = jnp.concatenate([jnp.where(mask, -1.0, 0.0) for mask in chosen] * 2, axis=1)
+    minus = jnp.concatenate([minus, jnp.zeros((dims, queries), jnp.float32)], axis=1)
+    free = jnp.concatenate(
+        [jnp.zeros((dims, 2 * LIMITED * queries), jnp.float32), jnp.where(limited, 0.0, 1.0)],
+        axis=1,
+    )
+    wide = jnp.concatenate(ends + [jnp.zeros((1, queries), jnp.float32)], axis=1)
+    end_rows = jnp.zeros((16, wide.shape[1]), jnp.float32)
+    place = lax.broadcasted_iota(jnp.int32, (16, 1), 0)
+    for p, part in enumerate(split(wide, 3)):
+        end_rows = jnp.where(place == p, part.astype(jnp.float32), end_rows)
     right = jnp.concatenate(
-        [jnp.concatenate(ones + [none], axis=1)] * 3
-        + [jnp.concatenate([none] * LIMITED + [free], axis=1)] * 3,
+        [minus.astype(jnp.bfloat16)] * 3
+        + [end_rows.astype(jnp.bfloat16)]
+        + [free.astype(jnp.bfloat16)] * 3,
         axis=0,
     )
+    ones = jnp.ones((16, per_piece * width), jnp.bfloat16)
 
     def step(picked, sums):
-        others = jnp.exp2(picked[:, LIMITED * queries :])
-        mass, slope = [], []
-        for k in range(LIMITED):
-            points = picked[:, k * queries : (k + 1) * queries]
-            m, s = box_terms(low_at[k] - points, high_at[k] - points)
-            mass.append(m)
-            slope.append(s)
+        at_block = lambda i: picked[:, i * queries : (i + 1) * queries]
+        others = jnp.exp2(at_block(2 * LIMITED))
+        mass, slope = zip(*[box_terms(at_block(k), at_block(LIMITED + k)) for k in range(LIMITED)])
         pair = others * mass[0]
-        last_two = pair * mass[1]
-        whole = last_two * mass[2]
-        return whole, (
-            sums[0] + whole,
-            sums[1] + (others * mass[1]) * (mass[2] * slope[0]),
-            sums[2] + pair * (mass[2] * slope[1]),
-            sums[3] + last_two * slope[2],
+        both = mass[1] * mass[2]
+        return pair * both, (
+            sums[0] + (others * slope[0]) * both,
+            sums[1] + pair * (mass[2] * slope[1]),
+            sums[2] + pair * (mass[1] * slope[2]),
         )
 
     def piece(start, totals):
@@ -122,9 +125,12 @@
             ],
             axis=0,
         )
-        full, slope = box_terms(-x, float(GRID) * unit - x)
-        ratio = jnp.concatenate(split(slope / full, 2), axis=0)
-        left = jnp.concatenate(split(x, 3) + split(jnp.log(0.5 * full) * LOG2_E, 3), axis=0)
+        rest = float(GRID) * unit - x
+        full = lax.erf(rest) + lax.erf(x)
+        slope = x * jnp.exp2((x * x) * -LOG2_E) + rest * jnp.exp2((rest * rest) * -LOG2_E)
+        ratio = jnp.concatenate(split(-slope / full, 2) + [ones], axis=0)
+        logs = jnp.log(0.5 * full) * LOG2_E
+        left = jnp.concatenate(split(x, 3) + [ones] + split(logs, 3), axis=0)
         picked = lax.dot_general(
             left, right, (((0,), (0,)), ((), ())), preferred_element_type=jnp.float32
         )
@@ -142,19 +148,21 @@
         return totals
 
     zero = jnp.zeros((16, queries), jnp.float32)
-    totals = (zero,) * (1 + LIMITED) + (jnp.zeros((2 * dims, 2 * queries), jnp.float32),)
+    totals = (zero,) * LIMITED + (jnp.zeros((2 * dims + 16, 2 * queries), jnp.float32),)
     if count == group:
         totals = pieces(0, totals)
     else:
         totals = lax.fori_loop(0, count // group, pieces, totals)
     sums = [jnp.sum(s, axis=0, keepdims=True) for s in totals[:-1]]
     products = totals[-1]
-    deriv = products[:dims, :queries] + (products[dims:, :queries] + products[:dims, queries:])
+    deriv = products[:dims, :queries]
+    deriv = deriv + (products[dims : 2 * dims, :queries] + products[:dims, queries:])
+    total = products[2 * dims : 2 * dims + 8, :queries] + products[2 * dims : 2 * dims + 8, queries:]
     deriv = jnp.where(limited, 0.0, deriv * (SLOPE / 4))
-    for mask, s in zip(chosen, sums[1:]):
+    for mask, s in zip(chosen, sums):
         deriv = jnp.where(mask, s * (SLOPE / 4), deriv)
     out_ref[:dims, :] = deriv
-    out_ref[dims:, :] = jnp.broadcast_to(sums[0] * 0.125, (8, queries))
+    out_ref[dims:, :] = total * 0.125
 
 
 def finish_kernel(sample_total, query_total, *refs):

time: 25.6 us -> 25.8 us (level)
  no operation moved by 1% of the time
where the time goes in v6:
time: 25.8 us; the launch traced here: 25.3 us
  blocking collectives  20.1 us (78%)
  Pallas kernels  2.71 us (11%)
  starting transfers between devices  1.01 us (4%)
  waiting for transfers between devices  0.84 us (3%)
  between operations  0.66 us (3%)
    all_to_all x2, blocking collectives, on_device(): lax.all_to_all(x, ('blk', 'grp'), 0, 0, axis_index_groups=groups)  20.1 us
    pallas_call x4, Pallas kernels, call(): pl.pallas_call(kernel, out_shape=outs[0] if single else outs, in_specs=[p...  2.71 us
    ppermute x1, starting transfers between devices, everyone(): lax.ppermute(x, axis, [(i, i ^ offset) for i in range(size)])  1.01 us
    ppermute x1, waiting for transfers between devices, everyone(): lax.ppermute(x, axis, [(i, i ^ offset) for i in range(size)])  0.84 us
  transfers between devices with their start and end apart: 1, of which 1 were waited for; matrix products, arithmetic and copies ran while one was open for 0% of the time, Pallas kernels for 0%

profile of v6, /device:TPU:0, one launch (start us, length us, event | category | flops | bytes accessed | tf_op | source)
XLA Modules:
  0.0 25.3 jit_solution(4267274473847798339)
XLA Ops:
  0.6 0.8 %shard_map.59 = (f32[16,8,128]{2,1,0:T(8,128)S(1)}, s32[2,32,128]{2,1,0:T(8,128)S(1)}, f32[1,32]{1,0:T(1,128)S(1)}, f32[1,128]{1,0:T(1,128)S(1)}) custom-call(f32[32,32]{1,0:T(8,128)} %x_ref.1, s32[2,32,128]{2,1,0:T(8,128)} %bounds_ref.1, f32[1,32]{1,0:T(1,128)} %bitcast.2, s32[1,128]{1,0:T(1,128)} %bitcast.3), custom_call_target="tpu_custom_call" | custom-call | tf_op jit(solution)/shard_map/pallas_call | solution.py:199
  1.5 11.2 %all_to_all.10.blocks_ref = f32[16,8,128]{2,1,0:T(8,128)S(1)} all-to-all(f32[16,8,128]{2,1,0:T(8,128)S(1)} %get-tuple-element.8), channel_id=1, replica_groups={{30,28,26,24,22,20,18,16,14,12,10,8,6,4,2,1},{31,29,27,25,23,21,19,17,1..., dimensions={0} | all-to-all | bytes 131072 | tf_op jit(solution)/shard_map/all_to_all | solution.py:243
  12.7 1.2 %shard_map.60.refs_0_ = f32[40,128]{1,0:T(8,128)S(1)} custom-call(f32[16,8,128]{2,1,0:T(8,128)S(1)} %all_to_all.10.blocks_ref, s32[2,32,128]{2,1,0:T(8,128)S(1)} %get-tuple-element.9.bounds_ref, f32[1,32]{1,0:T(1,128)S(1)} %get-tuple-element.10.spread_ref), custom_call_target="tpu_custom_call" | custom-call | tf_op jit(solution)/shard_map/pallas_call | solution.py:199
  13.9 1.0 %collective-permute-start = (f32[40,128]{1,0:T(8,128)S(1)}, f32[40,128]{1,0:T(8,128)S(1)}, u32[]{:S(2)}, u32[]{:S(2)}) collective-permute-start(f32[40,128]{1,0:T(8,128)S(1)} %shard_map.60.refs_0_), channel_id=1, source_target_pairs={{0,1},{1,0},{2,3},{3,2},{4,5},{5,4},{6,7},{7,6},{8,9},{9,8},{10,11... | collective-permute-start | bytes 61448 | tf_op jit(solution)/shard_map/ppermute | solution.py:193
  14.9 0.8 %collective-permute-done.refs_1_ = f32[40,128]{1,0:T(8,128)S(1)} collective-permute-done((f32[40,128]{1,0:T(8,128)S(1)}, f32[40,128]{1,0:T(8,128)S(1)}, u32[]{:S(2)}, u32[]{:S(2)}) %collective-permute-start) | collective-permute-done | bytes 20512 | tf_op jit(solution)/shard_map/ppermute | solution.py:193
  15.8 0.1 shard_map.61
  15.9 8.9 %all_to_all.11.shares_ref = f32[16,1,128]{2,1,0:T(1,128)S(1)} all-to-all(f32[16,1,128]{2,1,0:T(1,128)S(1)} %get-tuple-element.12), channel_id=1, replica_groups={{30,28,26,24,22,20,18,16,14,12,10,8,6,4,2,1},{31,29,27,25,23,21,19,17,1..., dimensions={0} | all-to-all | bytes 16384 | tf_op jit(solution)/shard_map/all_to_all | solution.py:243
  24.8 0.5 %shard_map.62 = (f32[128]{0:T(128)}, f32[32]{0:T(128)}) custom-call(f32[16,1,128]{2,1,0:T(1,128)S(1)} %all_to_all.11.shares_ref, f32[1,128]{1,0:T(1,128)S(1)} %get-tuple-element.13.held_log_ref), custom_call_target="tpu_custom_call" | custom-call | tf_op jit(solution)/shard_map/pallas_call | solution.py:199
Async XLA Ops:
  13.9 1.9 %collective-permute-start = (f32[40,128]{1,0:T(8,128)S(1)}, f32[40,128]{1,0:T(8,128)S(1)}, u32[]{:S(2)}, u32[]{:S(2)}) collective-permute-start(f32[40,128]{1,0:T(8,128)S(1)} %shard_map.60.refs_0_), channel_id=1, source_target_pairs={{0,1},{1,0},{2,3},{3,2},{4,5},{5,4},{6,7},{7,6},{8,9},{9,8},{10,11... | collective-permute-start | bytes 61448 | tf_op jit(solution)/shard_map/ppermute | solution.py:193

commit v7 on v1

--- a/solution.py
+++ b/solution.py
@@ -112,8 +112,7 @@
             sums[3] + last_two * slope[2],
         )
 
-    def piece(start, totals):
-        sums, products = totals[:-1], totals[-1]
+    def selection(start):
         some = [blocks_ref[start + b] for b in range(per_piece)]
         x = unit * jnp.concatenate(
             [
@@ -128,18 +127,25 @@
         picked = lax.dot_general(
             left, right, (((0,), (0,)), ((), ())), preferred_element_type=jnp.float32
         )
-        inside = []
-        for at_row in range(0, per_piece * width, 16):
-            whole, sums = step(picked[at_row : at_row + 16], sums)
-            inside.append(jnp.concatenate(split(whole, 2), axis=1))
-        inside = jnp.concatenate(inside, axis=0)
-        products = products + jnp.dot(ratio, inside, preferred_element_type=jnp.float32)
+        return picked, ratio
+
+    def pieces(number, totals):
+        sums, products = totals[:-1], totals[-1]
+        starts = [number * group + start for start in range(0, group, per_piece)]
+        ahead, behind = selection(starts[0]), None
+        for i in range(len(starts)):
+            picked, ratio = ahead
+            if i + 1 < len(starts):
+                ahead = selection(starts[i + 1])
+            if behind is not None:
+                products = products + jnp.dot(*behind, preferred_element_type=jnp.float32)
+            inside = []
+            for at_row in range(0, per_piece * width, 16):
+                whole, sums = step(picked[at_row : at_row + 16], sums)
+                inside.append(jnp.concatenate(split(whole, 2), axis=1))
+            behind = ratio, jnp.concatenate(inside, axis=0)
+        products = products + jnp.dot(*behind, preferred_element_type=jnp.float32)
         return (*sums, products)
-
-    def pieces(number, totals):
-        for start in range(0, group, per_piece):
-            totals = piece(number * group + start, totals)
-        return totals
 
     zero = jnp.zeros((16, queries), jnp.float32)
     totals = (zero,) * (1 + LIMITED) + (jnp.zeros((2 * dims, 2 * queries), jnp.float32),)

time: 25.6 us -> 25.6 us (level)
  no operation moved by 1% of the time
where the time goes in v7:
time: 25.6 us; the launch traced here: 25.1 us
  blocking collectives  20.1 us (79%)
  Pallas kernels  2.52 us (10%)
  starting transfers between devices  1.01 us (4%)
  waiting for transfers between devices  0.84 us (3%)
  between operations  0.66 us (3%)
    all_to_all x2, blocking collectives, on_device(): lax.all_to_all(x, ('blk', 'grp'), 0, 0, axis_index_groups=groups)  20.1 us
    pallas_call x4, Pallas kernels, call(): pl.pallas_call(kernel, out_shape=outs[0] if single else outs, in_specs=[p...  2.52 us
    ppermute x1, starting transfers between devices, everyone(): lax.ppermute(x, axis, [(i, i ^ offset) for i in range(size)])  1.01 us
    ppermute x1, waiting for transfers between devices, everyone(): lax.ppermute(x, axis, [(i, i ^ offset) for i in range(size)])  0.84 us
  transfers between devices with their start and end apart: 1, of which 1 were waited for; matrix products, arithmetic and copies ran while one was open for 0% of the time, Pallas kernels for 0%

profile of v7, /device:TPU:0, one launch (start us, length us, event | category | flops | bytes accessed | tf_op | source)
XLA Modules:
  0.0 25.1 jit_solution(7076649080659000834)
XLA Ops:
  0.6 0.8 %shard_map.59 = (f32[16,8,128]{2,1,0:T(8,128)S(1)}, s32[2,32,128]{2,1,0:T(8,128)S(1)}, f32[1,32]{1,0:T(1,128)S(1)}, f32[1,128]{1,0:T(1,128)S(1)}) custom-call(f32[32,32]{1,0:T(8,128)} %x_ref.1, s32[2,32,128]{2,1,0:T(8,128)} %bounds_ref.1, f32[1,32]{1,0:T(1,128)} %bitcast.2, s32[1,128]{1,0:T(1,128)} %bitcast.3), custom_call_target="tpu_custom_call" | custom-call | tf_op jit(solution)/shard_map/pallas_call | solution.py:197
  1.5 11.2 %all_to_all.10.blocks_ref = f32[16,8,128]{2,1,0:T(8,128)S(1)} all-to-all(f32[16,8,128]{2,1,0:T(8,128)S(1)} %get-tuple-element.8), channel_id=1, replica_groups={{30,28,26,24,22,20,18,16,14,12,10,8,6,4,2,1},{31,29,27,25,23,21,19,17,1..., dimensions={0} | all-to-all | bytes 131072 | tf_op jit(solution)/shard_map/all_to_all | solution.py:241
  12.7 1.0 %shard_map.60.refs_0_ = f32[40,128]{1,0:T(8,128)S(1)} custom-call(f32[16,8,128]{2,1,0:T(8,128)S(1)} %all_to_all.10.blocks_ref, s32[2,32,128]{2,1,0:T(8,128)S(1)} %get-tuple-element.9.bounds_ref, f32[1,32]{1,0:T(1,128)S(1)} %get-tuple-element.10.spread_ref), custom_call_target="tpu_custom_call" | custom-call | tf_op jit(solution)/shard_map/pallas_call | solution.py:197
  13.7 1.0 %collective-permute-start = (f32[40,128]{1,0:T(8,128)S(1)}, f32[40,128]{1,0:T(8,128)S(1)}, u32[]{:S(2)}, u32[]{:S(2)}) collective-permute-start(f32[40,128]{1,0:T(8,128)S(1)} %shard_map.60.refs_0_), channel_id=1, source_target_pairs={{0,1},{1,0},{2,3},{3,2},{4,5},{5,4},{6,7},{7,6},{8,9},{9,8},{10,11... | collective-permute-start | bytes 61448 | tf_op jit(solution)/shard_map/ppermute | solution.py:191
  14.7 0.8 %collective-permute-done.refs_1_ = f32[40,128]{1,0:T(8,128)S(1)} collective-permute-done((f32[40,128]{1,0:T(8,128)S(1)}, f32[40,128]{1,0:T(8,128)S(1)}, u32[]{:S(2)}, u32[]{:S(2)}) %collective-permute-start) | collective-permute-done | bytes 20512 | tf_op jit(solution)/shard_map/ppermute | solution.py:191
  15.6 0.1 shard_map.61
  15.7 8.9 %all_to_all.11.shares_ref = f32[16,1,128]{2,1,0:T(1,128)S(1)} all-to-all(f32[16,1,128]{2,1,0:T(1,128)S(1)} %get-tuple-element.12), channel_id=1, replica_groups={{30,28,26,24,22,20,18,16,14,12,10,8,6,4,2,1},{31,29,27,25,23,21,19,17,1..., dimensions={0} | all-to-all | bytes 16384 | tf_op jit(solution)/shard_map/all_to_all | solution.py:241
  24.6 0.5 %shard_map.62 = (f32[128]{0:T(128)}, f32[32]{0:T(128)}) custom-call(f32[16,1,128]{2,1,0:T(1,128)S(1)} %all_to_all.11.shares_ref, f32[1,128]{1,0:T(1,128)S(1)} %get-tuple-element.13.held_log_ref), custom_call_target="tpu_custom_call" | custom-call | tf_op jit(solution)/shard_map/pallas_call | solution.py:197
Async XLA Ops:
  13.7 1.9 %collective-permute-start = (f32[40,128]{1,0:T(8,128)S(1)}, f32[40,128]{1,0:T(8,128)S(1)}, u32[]{:S(2)}, u32[]{:S(2)}) collective-permute-start(f32[40,128]{1,0:T(8,128)S(1)} %shard_map.60.refs_0_), channel_id=1, source_target_pairs={{0,1},{1,0},{2,3},{3,2},{4,5},{5,4},{6,7},{7,6},{8,9},{9,8},{10,11... | collective-permute-start | bytes 61448 | tf_op jit(solution)/shard_map/ppermute | solution.py:191

commit v8 on v4

--- a/solution.py
+++ b/solution.py
@@ -86,17 +86,22 @@
     high = high.astype(jnp.float32) * unit
     low_at = [pick(mask, low) for mask in chosen]
     high_at = [pick(mask, high) for mask in chosen]
-
-    as_ones = lambda mask: jnp.where(mask, 1.0, 0.0).astype(jnp.bfloat16)
-    one_hot = jnp.concatenate([as_ones(mask) for mask in chosen], axis=1)
-    one_hot = jnp.concatenate([one_hot] * pieces, axis=0)
-    free = jnp.concatenate([as_ones(jnp.logical_not(limited))] * pieces, axis=0)
-
-    def step(boxes, others, sums):
-        others = jnp.exp2(others)
+    second = jnp.sum(jnp.where(chosen[1], at, 0), axis=0, keepdims=True)
+    lane_of = [
+        [jnp.broadcast_to(dim + dims * j, (16, queries)) for dim in (first, second, last)]
+        for j in range(pieces)
+    ]
+    place = lambda axis: lax.broadcasted_iota(jnp.int32, (lanes, lanes), axis) // dims
+    same = jnp.where(place(0) == place(1), 1.0, 0.0).astype(jnp.bfloat16)
+
+    def step(x, minus_log, rest_log, lane_at, sums):
+        take = lambda values, k: jnp.take_along_axis(
+            values, lane_at[k], axis=1, mode="promise_in_bounds"
+        )
+        others = jnp.exp2(take(minus_log, 0) + take(minus_log, 1) + take(rest_log, 2))
         mass, slope = [], []
         for k in range(LIMITED):
-            points = boxes[:, k * queries : (k + 1) * queries]
+            points = take(x, k)
             m, s = box_terms(low_at[k] - points, high_at[k] - points)
             mass.append(m)
             slope.append(s)
@@ -110,33 +115,23 @@
             sums[3] + last_two * slope[2],
         )
 
-    place = lax.broadcasted_iota(jnp.int32, (1, lanes), 1) // dims
-
-    def thirds(x):
-        head = x.astype(jnp.bfloat16).astype(jnp.float32)
-        rest = x - head
-        tail = rest - rest.astype(jnp.bfloat16).astype(jnp.float32)
-        return [x, pltpu.roll(rest, dims, 1), pltpu.roll(tail, 2 * dims, 1)]
-
-    def left(parts, j):
-        x = jnp.zeros_like(parts[0])
-        for p, part in enumerate(parts):
-            x = jnp.where(place == (j + p) % pieces, part, x)
-        return x.astype(jnp.bfloat16)
-
     def chunk(number, totals):
         sums, products = totals[:-1], totals[-1]
         x = blocks_ref[pl.ds(number * group, group)].reshape(128, lanes) * unit_row
-        points = thirds(x)
         full, slope = box_terms(-x, float(GRID) * unit_row - x)
-        logs = thirds(jnp.log(0.5 * full) * LOG2_E)
+        logs = jnp.log(0.5 * full) * LOG2_E
+        every = jnp.dot(
+            jnp.concatenate(split(logs, 3), axis=1),
+            jnp.concatenate([same] * 3, axis=0),
+            preferred_element_type=jnp.float32,
+        )
+        rest_log = every - logs
         ratio = split((slope / full).T, 2)
         for j in range(pieces):
-            boxes = jnp.dot(left(points, j), one_hot, preferred_element_type=jnp.float32)
-            others = jnp.dot(left(logs, j), free, preferred_element_type=jnp.float32)
             inside = []
             for r in range(0, 128, 16):
-                whole, sums = step(boxes[r : r + 16], others[r : r + 16], sums)
+                rows = slice(r, r + 16)
+                whole, sums = step(x[rows], -logs[rows], rest_log[rows], lane_of[j], sums)
                 inside.append(jnp.concatenate(split(whole, 2), axis=1))
             ratio_at = jnp.concatenate([part[j * dims : (j + 1) * dims] for part in ratio], axis=0)
             products = products + jnp.dot(

time: 25.8 us -> 25.9 us (level)
  no operation moved by 1% of the time
where the time goes in v8:
time: 25.9 us; the launch traced here: 25.4 us
  blocking collectives  20.1 us (78%)
  Pallas kernels  2.83 us (11%)
  starting transfers between devices  1.01 us (4%)
  waiting for transfers between devices  0.84 us (3%)
  between operations  0.65 us (3%)
    all_to_all x2, blocking collectives, on_device(): lax.all_to_all(x, ('blk', 'grp'), 0, 0, axis_index_groups=groups)  20.1 us
    pallas_call x4, Pallas kernels, call(): pl.pallas_call(kernel, out_shape=outs[0] if single else outs, in_specs=[p...  2.83 us
    ppermute x1, starting transfers between devices, everyone(): lax.ppermute(x, axis, [(i, i ^ offset) for i in range(size)])  1.01 us
    ppermute x1, waiting for transfers between devices, everyone(): lax.ppermute(x, axis, [(i, i ^ offset) for i in range(size)])  0.84 us
  transfers between devices with their start and end apart: 1, of which 1 were waited for; matrix products, arithmetic and copies ran while one was open for 0% of the time, Pallas kernels for 0%

profile of v8, /device:TPU:0, one launch (start us, length us, event | category | flops | bytes accessed | tf_op | source)
XLA Modules:
  0.0 25.4 jit_solution(351778209444978538)
XLA Ops:
  0.6 0.9 %shard_map.59 = (f32[16,8,128]{2,1,0:T(8,128)S(1)}, s32[2,32,128]{2,1,0:T(8,128)S(1)}, f32[1,32]{1,0:T(1,128)S(1)}, f32[1,128]{1,0:T(1,128)S(1)}) custom-call(f32[32,32]{1,0:T(8,128)} %x_ref.1, s32[2,32,128]{2,1,0:T(8,128)} %bounds_ref.1, f32[1,32]{1,0:T(1,128)} %bitcast.2, s32[1,128]{1,0:T(1,128)} %bitcast.3), custom_call_target="tpu_custom_call" | custom-call | tf_op jit(solution)/shard_map/pallas_call | solution.py:187
  1.6 11.2 %all_to_all.10.blocks_ref = f32[16,8,128]{2,1,0:T(8,128)S(1)} all-to-all(f32[16,8,128]{2,1,0:T(8,128)S(1)} %get-tuple-element.8), channel_id=1, replica_groups={{30,28,26,24,22,20,18,16,14,12,10,8,6,4,2,1},{31,29,27,25,23,21,19,17,1..., dimensions={0} | all-to-all | bytes 131072 | tf_op jit(solution)/shard_map/all_to_all | solution.py:231
  12.8 1.3 %shard_map.60.refs_0_ = f32[40,128]{1,0:T(8,128)S(1)} custom-call(f32[16,8,128]{2,1,0:T(8,128)S(1)} %all_to_all.10.blocks_ref, s32[2,32,128]{2,1,0:T(8,128)S(1)} %get-tuple-element.9.bounds_ref, f32[1,32]{1,0:T(1,128)S(1)} %get-tuple-element.10.spread_ref), custom_call_target="tpu_custom_call" | custom-call | tf_op jit(solution)/shard_map/pallas_call | solution.py:187
  14.0 1.0 %collective-permute-start = (f32[40,128]{1,0:T(8,128)S(1)}, f32[40,128]{1,0:T(8,128)S(1)}, u32[]{:S(2)}, u32[]{:S(2)}) collective-permute-start(f32[40,128]{1,0:T(8,128)S(1)} %shard_map.60.refs_0_), channel_id=1, source_target_pairs={{0,1},{1,0},{2,3},{3,2},{4,5},{5,4},{6,7},{7,6},{8,9},{9,8},{10,11... | collective-permute-start | bytes 61448 | tf_op jit(solution)/shard_map/ppermute | solution.py:181
  15.1 0.8 %collective-permute-done.refs_1_ = f32[40,128]{1,0:T(8,128)S(1)} collective-permute-done((f32[40,128]{1,0:T(8,128)S(1)}, f32[40,128]{1,0:T(8,128)S(1)}, u32[]{:S(2)}, u32[]{:S(2)}) %collective-permute-start) | collective-permute-done | bytes 20512 | tf_op jit(solution)/shard_map/ppermute | solution.py:181
  15.9 0.1 shard_map.61
  16.0 8.9 %all_to_all.11.shares_ref = f32[16,1,128]{2,1,0:T(1,128)S(1)} all-to-all(f32[16,1,128]{2,1,0:T(1,128)S(1)} %get-tuple-element.12), channel_id=1, replica_groups={{30,28,26,24,22,20,18,16,14,12,10,8,6,4,2,1},{31,29,27,25,23,21,19,17,1..., dimensions={0} | all-to-all | bytes 16384 | tf_op jit(solution)/shard_map/all_to_all | solution.py:231
  24.9 0.5 %shard_map.62 = (f32[128]{0:T(128)}, f32[32]{0:T(128)}) custom-call(f32[16,1,128]{2,1,0:T(1,128)S(1)} %all_to_all.11.shares_ref, f32[1,128]{1,0:T(1,128)S(1)} %get-tuple-element.13.held_log_ref), custom_call_target="tpu_custom_call" | custom-call | tf_op jit(solution)/shard_map/pallas_call | solution.py:187
Async XLA Ops:
  14.0 1.9 %collective-permute-start = (f32[40,128]{1,0:T(8,128)S(1)}, f32[40,128]{1,0:T(8,128)S(1)}, u32[]{:S(2)}, u32[]{:S(2)}) collective-permute-start(f32[40,128]{1,0:T(8,128)S(1)} %shard_map.60.refs_0_), channel_id=1, source_target_pairs={{0,1},{1,0},{2,3},{3,2},{4,5},{5,4},{6,7},{7,6},{8,9},{9,8},{10,11... | collective-permute-start | bytes 61448 | tf_op jit(solution)/shard_map/ppermute | solution.py:181

commit v9 on v1

--- a/solution.py
+++ b/solution.py
@@ -39,8 +39,8 @@
 
 def load_kernel(
     x_ref, bounds_ref, spread_ref, counts_ref,
-    out_ref, held_bounds, held_spread, target_ref,
-    held_x, held_counts, sems,
+    out_ref, held_bounds, held_spread, held_counts,
+    held_x, sems,
 ):
     sources = (x_ref, bounds_ref, spread_ref, counts_ref)
     targets = (held_x, held_bounds, held_spread, held_counts)
@@ -57,8 +57,6 @@
         out_ref[peer] = packed
     for copy in copies[1:]:
         copy.wait()
-    smoothing = 1.0 / TABLE_ROWS
-    target_ref[...] = jnp.log(held_counts[...].astype(jnp.float32) / TABLE_ROWS + smoothing)
 
 
 def terms_kernel(width, blocks_ref, bounds_ref, spread_ref, out_ref):
@@ -93,6 +91,8 @@
         + [jnp.concatenate([none] * LIMITED + [free], axis=1)] * 3,
         axis=0,
     )
+
+    ones = jnp.ones((16, per_piece * width), jnp.bfloat16)
 
     def step(picked, sums):
         others = jnp.exp2(picked[:, LIMITED * queries :])
@@ -106,10 +106,9 @@
         last_two = pair * mass[1]
         whole = last_two * mass[2]
         return whole, (
-            sums[0] + whole,
-            sums[1] + (others * mass[1]) * (mass[2] * slope[0]),
-            sums[2] + pair * (mass[2] * slope[1]),
-            sums[3] + last_two * slope[2],
+            sums[0] + (others * mass[1]) * (mass[2] * slope[0]),
+            sums[1] + pair * (mass[2] * slope[1]),
+            sums[2] + last_two * slope[2],
         )
 
     def piece(start, totals):
@@ -122,8 +121,10 @@
             ],
             axis=0,
         )
-        full, slope = box_terms(-x, float(GRID) * unit - x)
-        ratio = jnp.concatenate(split(slope / full, 2), axis=0)
+        rest = float(GRID) * unit - x
+        full = lax.erf(rest) + lax.erf(x)
+        slope = x * jnp.exp2((x * x) * -LOG2_E) + rest * jnp.exp2((rest * rest) * -LOG2_E)
+        ratio = jnp.concatenate(split(-slope / full, 2) + [ones], axis=0)
         left = jnp.concatenate(split(x, 3) + split(jnp.log(0.5 * full) * LOG2_E, 3), axis=0)
         picked = lax.dot_general(
             left, right, (((0,), (0,)), ((), ())), preferred_element_type=jnp.float32
@@ -142,30 +143,33 @@
         return totals
 
     zero = jnp.zeros((16, queries), jnp.float32)
-    totals = (zero,) * (1 + LIMITED) + (jnp.zeros((2 * dims, 2 * queries), jnp.float32),)
+    totals = (zero,) * LIMITED + (jnp.zeros((2 * dims + 16, 2 * queries), jnp.float32),)
     if count == group:
         totals = pieces(0, totals)
     else:
         totals = lax.fori_loop(0, count // group, pieces, totals)
     sums = [jnp.sum(s, axis=0, keepdims=True) for s in totals[:-1]]
     products = totals[-1]
-    deriv = products[:dims, :queries] + (products[dims:, :queries] + products[:dims, queries:])
+    deriv = products[dims : 2 * dims, :queries] + products[:dims, queries:]
+    deriv = products[:dims, :queries] + deriv
+    total = products[2 * dims : 2 * dims + 8, :queries] + products[2 * dims : 2 * dims + 8, queries:]
     deriv = jnp.where(limited, 0.0, deriv * (SLOPE / 4))
-    for mask, s in zip(chosen, sums[1:]):
+    for mask, s in zip(chosen, sums):
         deriv = jnp.where(mask, s * (SLOPE / 4), deriv)
     out_ref[:dims, :] = deriv
-    out_ref[dims:, :] = jnp.broadcast_to(sums[0] * 0.125, (8, queries))
+    out_ref[dims:, :] = total * 0.125
 
 
 def finish_kernel(sample_total, query_total, *refs):
-    part_refs, (target_ref, log_ref, share_ref) = refs[:-3], refs[-3:]
+    part_refs, (counts_ref, log_ref, share_ref) = refs[:-3], refs[-3:]
     whole = tree_sum([ref[...] for ref in part_refs])
     dims, queries = whole.shape[0] - 8, whole.shape[1]
     smoothing = 1.0 / TABLE_ROWS
     estimate = whole[dims : dims + 1] / sample_total
     log_est = jnp.log(estimate + smoothing)
     log_ref[...] = log_est
-    weight = 2.0 * (log_est - target_ref[...]) / (query_total * (estimate + smoothing))
+    target = jnp.log(counts_ref[...].astype(jnp.float32) / TABLE_ROWS + smoothing)
+    weight = 2.0 * (log_est - target) / (query_total * (estimate + smoothing))
     terms = whole[:dims] * (weight / sample_total)
     terms = jnp.concatenate([terms, jnp.zeros((queries - dims, queries), jnp.float32)], axis=0)
     share = jnp.sum(terms.T, axis=0, keepdims=True)
@@ -211,8 +215,7 @@
     sample_total = width * blocks * copies
     query_total = queries * blocks
 
-    counts_vector = pltpu.VMEM((1, queries), jnp.int32)
-    packed, bounds, spread, target = call(
+    packed, bounds, spread, counts = call(
         load_kernel,
         [
             pltpu.with_memory_space_constraint(array, pltpu.HBM)
@@ -222,9 +225,9 @@
             pltpu.VMEM((blocks, 8, dims * width // 8), jnp.float32),
             pltpu.VMEM(bounds.shape, bounds.dtype),
             pltpu.VMEM((1, dims), jnp.float32),
-            pltpu.VMEM((1, queries), jnp.float32),
+            pltpu.VMEM((1, queries), jnp.int32),
         ],
-        [pltpu.VMEM((dims, width), jnp.float32), counts_vector, pltpu.SemaphoreType.DMA((4,))],
+        [pltpu.VMEM((dims, width), jnp.float32), pltpu.SemaphoreType.DMA((4,))],
         placed=pl.ANY,
     )
     turned = [1] + [0] * (blocks - 1)
@@ -241,7 +244,7 @@
     )
     log_est, share = call(
         functools.partial(finish_kernel, sample_total, query_total),
-        everyone(part, "grp") + [target],
+        everyone(part, "grp") + [counts],
         [shape(1, queries), shape(blocks, 1, queries)],
     )
     shares = exchange(share)

time: 25.6 us -> 25.6 us (level)
  no operation moved by 1% of the time
where the time goes in v9:
time: 25.6 us; the launch traced here: 25.1 us
  blocking collectives  20.1 us (79%)
  Pallas kernels  2.49 us (10%)
  starting transfers between devices  1.01 us (4%)
  waiting for transfers between devices  0.84 us (3%)
  between operations  0.66 us (3%)
    all_to_all x2, blocking collectives, on_device(): lax.all_to_all(x, ('blk', 'grp'), 0, 0, axis_index_groups=groups)  20.1 us
    pallas_call x4, Pallas kernels, call(): pl.pallas_call(kernel, out_shape=outs[0] if single else outs, in_specs=[p...  2.49 us
    ppermute x1, starting transfers between devices, everyone(): lax.ppermute(x, axis, [(i, i ^ offset) for i in range(size)])  1.01 us
    ppermute x1, waiting for transfers between devices, everyone(): lax.ppermute(x, axis, [(i, i ^ offset) for i in range(size)])  0.84 us
  transfers between devices with their start and end apart: 1, of which 1 were waited for; matrix products, arithmetic and copies ran while one was open for 0% of the time, Pallas kernels for 0%

profile of v9, /device:TPU:0, one launch (start us, length us, event | category | flops | bytes accessed | tf_op | source)
XLA Modules:
  0.0 25.1 jit_solution(9518387996949934745)
XLA Ops:
  0.6 0.8 %shard_map.59 = (f32[16,8,128]{2,1,0:T(8,128)S(1)}, s32[2,32,128]{2,1,0:T(8,128)S(1)}, f32[1,32]{1,0:T(1,128)S(1)}, s32[1,128]{1,0:T(1,128)S(1)}) custom-call(f32[32,32]{1,0:T(8,128)} %x_ref.1, s32[2,32,128]{2,1,0:T(8,128)} %bounds_ref.1, f32[1,32]{1,0:T(1,128)} %bitcast.2, s32[1,128]{1,0:T(1,128)} %bitcast.3), custom_call_target="tpu_custom_call" | custom-call | tf_op jit(solution)/shard_map/pallas_call | solution.py:195
  1.5 11.2 %all_to_all.10.blocks_ref = f32[16,8,128]{2,1,0:T(8,128)S(1)} all-to-all(f32[16,8,128]{2,1,0:T(8,128)S(1)} %get-tuple-element.8), channel_id=1, replica_groups={{30,28,26,24,22,20,18,16,14,12,10,8,6,4,2,1},{31,29,27,25,23,21,19,17,1..., dimensions={0} | all-to-all | bytes 131072 | tf_op jit(solution)/shard_map/all_to_all | solution.py:238
  12.7 1.0 %shard_map.60.refs_0_ = f32[40,128]{1,0:T(8,128)S(1)} custom-call(f32[16,8,128]{2,1,0:T(8,128)S(1)} %all_to_all.10.blocks_ref, s32[2,32,128]{2,1,0:T(8,128)S(1)} %get-tuple-element.9.bounds_ref, f32[1,32]{1,0:T(1,128)S(1)} %get-tuple-element.10.spread_ref), custom_call_target="tpu_custom_call" | custom-call | tf_op jit(solution)/shard_map/pallas_call | solution.py:195
  13.7 1.0 %collective-permute-start = (f32[40,128]{1,0:T(8,128)S(1)}, f32[40,128]{1,0:T(8,128)S(1)}, u32[]{:S(2)}, u32[]{:S(2)}) collective-permute-start(f32[40,128]{1,0:T(8,128)S(1)} %shard_map.60.refs_0_), channel_id=1, source_target_pairs={{0,1},{1,0},{2,3},{3,2},{4,5},{5,4},{6,7},{7,6},{8,9},{9,8},{10,11... | collective-permute-start | bytes 61448 | tf_op jit(solution)/shard_map/ppermute | solution.py:189
  14.7 0.8 %collective-permute-done.refs_1_ = f32[40,128]{1,0:T(8,128)S(1)} collective-permute-done((f32[40,128]{1,0:T(8,128)S(1)}, f32[40,128]{1,0:T(8,128)S(1)}, u32[]{:S(2)}, u32[]{:S(2)}) %collective-permute-start) | collective-permute-done | bytes 20512 | tf_op jit(solution)/shard_map/ppermute | solution.py:189
  15.6 0.1 shard_map.61
  15.7 8.9 %all_to_all.11.shares_ref = f32[16,1,128]{2,1,0:T(1,128)S(1)} all-to-all(f32[16,1,128]{2,1,0:T(1,128)S(1)} %get-tuple-element.12), channel_id=1, replica_groups={{30,28,26,24,22,20,18,16,14,12,10,8,6,4,2,1},{31,29,27,25,23,21,19,17,1..., dimensions={0} | all-to-all | bytes 16384 | tf_op jit(solution)/shard_map/all_to_all | solution.py:238
  24.6 0.5 %shard_map.62 = (f32[128]{0:T(128)}, f32[32]{0:T(128)}) custom-call(f32[16,1,128]{2,1,0:T(1,128)S(1)} %all_to_all.11.shares_ref, f32[1,128]{1,0:T(1,128)S(1)} %get-tuple-element.13.held_log_ref), custom_call_target="tpu_custom_call" | custom-call | tf_op jit(solution)/shard_map/pallas_call | solution.py:195
Async XLA Ops:
  13.7 1.9 %collective-permute-start = (f32[40,128]{1,0:T(8,128)S(1)}, f32[40,128]{1,0:T(8,128)S(1)}, u32[]{:S(2)}, u32[]{:S(2)}) collective-permute-start(f32[40,128]{1,0:T(8,128)S(1)} %shard_map.60.refs_0_), channel_id=1, source_target_pairs={{0,1},{1,0},{2,3},{3,2},{4,5},{5,4},{6,7},{7,6},{8,9},{9,8},{10,11... | collective-permute-start | bytes 61448 | tf_op jit(solution)/shard_map/ppermute | solution.py:189

commit v10 on v9

--- a/solution.py
+++ b/solution.py
@@ -39,8 +39,8 @@
 
 def load_kernel(
     x_ref, bounds_ref, spread_ref, counts_ref,
-    out_ref, held_bounds, held_spread, held_counts,
-    held_x, sems,
+    out_ref, held_bounds, unit_ref, held_counts,
+    held_x, held_spread, sems,
 ):
     sources = (x_ref, bounds_ref, spread_ref, counts_ref)
     targets = (held_x, held_bounds, held_spread, held_counts)
@@ -57,9 +57,14 @@
         out_ref[peer] = packed
     for copy in copies[1:]:
         copy.wait()
-
-
-def terms_kernel(width, blocks_ref, bounds_ref, spread_ref, out_ref):
+    dims = held_spread.shape[1]
+    row = lax.broadcasted_iota(jnp.int32, (dims, dims), 0)
+    column = lax.broadcasted_iota(jnp.int32, (dims, dims), 1)
+    unit = jnp.where(row == column, ROOT_HALF / held_spread[...], 0.0)
+    unit_ref[...] = jnp.broadcast_to(jnp.sum(unit, axis=1, keepdims=True), unit_ref.shape)
+
+
+def terms_kernel(width, blocks_ref, bounds_ref, unit_ref, out_ref):
     dims, queries = bounds_ref.shape[1:]
     count = blocks_ref.shape[0]
     per_piece = 128 // width
@@ -72,10 +77,7 @@
     last = jnp.max(jnp.where(limited, at, -1), axis=0, keepdims=True)
     chosen = [at == first, limited & (at > first) & (at < last), at == last]
 
-    row = lax.broadcasted_iota(jnp.int32, (dims, dims), 0)
-    column = lax.broadcasted_iota(jnp.int32, (dims, dims), 1)
-    spread = jnp.sum(jnp.where(row == column, spread_ref[...], 0.0), axis=1, keepdims=True)
-    unit = ROOT_HALF / spread
+    unit = unit_ref[...]
 
     pick = lambda mask, values: jnp.sum(jnp.where(mask, values, 0.0), axis=0, keepdims=True)
     low = low.astype(jnp.float32) * unit
@@ -215,7 +217,7 @@
     sample_total = width * blocks * copies
     query_total = queries * blocks
 
-    packed, bounds, spread, counts = call(
+    packed, bounds, unit, counts = call(
         load_kernel,
         [
             pltpu.with_memory_space_constraint(array, pltpu.HBM)
@@ -224,10 +226,14 @@
         [
             pltpu.VMEM((blocks, 8, dims * width // 8), jnp.float32),
             pltpu.VMEM(bounds.shape, bounds.dtype),
-            pltpu.VMEM((1, dims), jnp.float32),
+            pltpu.VMEM((dims, queries), jnp.float32),
             pltpu.VMEM((1, queries), jnp.int32),
         ],
-        [pltpu.VMEM((dims, width), jnp.float32), pltpu.SemaphoreType.DMA((4,))],
+        [
+            pltpu.VMEM((dims, width), jnp.float32),
+            pltpu.VMEM((1, dims), jnp.float32),
+            pltpu.SemaphoreType.DMA((4,)),
+        ],
         placed=pl.ANY,
     )
     turned = [1] + [0] * (blocks - 1)
@@ -239,7 +245,7 @@
     gathered = exchange(packed)
     part = call(
         functools.partial(terms_kernel, width),
-        [gathered, bounds, spread],
+        [gathered, bounds, unit],
         [shape(dims + 8, queries)],
     )
     log_est, share = call(

time: 25.6 us -> 25.6 us (level)
  no operation moved by 1% of the time
where the time goes in v10:
time: 25.6 us; the launch traced here: 25.2 us
  blocking collectives  20.1 us (79%)
  Pallas kernels  2.56 us (10%)
  starting transfers between devices  1.01 us (4%)
  waiting for transfers between devices  0.84 us (3%)
  between operations  0.66 us (3%)
    all_to_all x2, blocking collectives, on_device(): lax.all_to_all(x, ('blk', 'grp'), 0, 0, axis_index_groups=groups)  20.1 us
    pallas_call x4, Pallas kernels, call(): pl.pallas_call(kernel, out_shape=outs[0] if single else outs, in_specs=[p...  2.56 us
    ppermute x1, starting transfers between devices, everyone(): lax.ppermute(x, axis, [(i, i ^ offset) for i in range(size)])  1.01 us
    ppermute x1, waiting for transfers between devices, everyone(): lax.ppermute(x, axis, [(i, i ^ offset) for i in range(size)])  0.84 us
  transfers between devices with their start and end apart: 1, of which 1 were waited for; matrix products, arithmetic and copies ran while one was open for 0% of the time, Pallas kernels for 0%

profile of v10, /device:TPU:0, one launch (start us, length us, event | category | flops | bytes accessed | tf_op | source)
XLA Modules:
  0.0 25.2 jit_solution(12980120871217848957)
XLA Ops:
  0.6 0.9 %shard_map.59 = (f32[16,8,128]{2,1,0:T(8,128)S(1)}, s32[2,32,128]{2,1,0:T(8,128)S(1)}, f32[32,128]{1,0:T(8,128)S(1)}, s32[1,128]{1,0:T(1,128)S(1)}) custom-call(f32[32,32]{1,0:T(8,128)} %x_ref.1, s32[2,32,128]{2,1,0:T(8,128)} %bounds_ref.1, f32[1,32]{1,0:T(1,128)} %bitcast.2, s32[1,128]{1,0:T(1,128)} %bitcast.3), custom_call_target="tpu_custom_call" | custom-call | tf_op jit(solution)/shard_map/pallas_call | solution.py:197
  1.6 11.2 %all_to_all.10.blocks_ref = f32[16,8,128]{2,1,0:T(8,128)S(1)} all-to-all(f32[16,8,128]{2,1,0:T(8,128)S(1)} %get-tuple-element.8), channel_id=1, replica_groups={{30,28,26,24,22,20,18,16,14,12,10,8,6,4,2,1},{31,29,27,25,23,21,19,17,1..., dimensions={0} | all-to-all | bytes 131072 | tf_op jit(solution)/shard_map/all_to_all | solution.py:244
  12.8 1.0 %shard_map.60.refs_0_ = f32[40,128]{1,0:T(8,128)S(1)} custom-call(f32[16,8,128]{2,1,0:T(8,128)S(1)} %all_to_all.10.blocks_ref, s32[2,32,128]{2,1,0:T(8,128)S(1)} %get-tuple-element.9.bounds_ref, f32[32,128]{1,0:T(8,128)S(1)} %get-tuple-element.10.unit_ref), custom_call_target="tpu_custom_call" | custom-call | tf_op jit(solution)/shard_map/pallas_call | solution.py:197
  13.8 1.0 %collective-permute-start = (f32[40,128]{1,0:T(8,128)S(1)}, f32[40,128]{1,0:T(8,128)S(1)}, u32[]{:S(2)}, u32[]{:S(2)}) collective-permute-start(f32[40,128]{1,0:T(8,128)S(1)} %shard_map.60.refs_0_), channel_id=1, source_target_pairs={{0,1},{1,0},{2,3},{3,2},{4,5},{5,4},{6,7},{7,6},{8,9},{9,8},{10,11... | collective-permute-start | bytes 61448 | tf_op jit(solution)/shard_map/ppermute | solution.py:191
  14.8 0.8 %collective-permute-done.refs_1_ = f32[40,128]{1,0:T(8,128)S(1)} collective-permute-done((f32[40,128]{1,0:T(8,128)S(1)}, f32[40,128]{1,0:T(8,128)S(1)}, u32[]{:S(2)}, u32[]{:S(2)}) %collective-permute-start) | collective-permute-done | bytes 20512 | tf_op jit(solution)/shard_map/ppermute | solution.py:191
  15.6 0.1 shard_map.61
  15.8 8.9 %all_to_all.11.shares_ref = f32[16,1,128]{2,1,0:T(1,128)S(1)} all-to-all(f32[16,1,128]{2,1,0:T(1,128)S(1)} %get-tuple-element.12), channel_id=1, replica_groups={{30,28,26,24,22,20,18,16,14,12,10,8,6,4,2,1},{31,29,27,25,23,21,19,17,1..., dimensions={0} | all-to-all | bytes 16384 | tf_op jit(solution)/shard_map/all_to_all | solution.py:244
  24.6 0.5 %shard_map.62 = (f32[128]{0:T(128)}, f32[32]{0:T(128)}) custom-call(f32[16,1,128]{2,1,0:T(1,128)S(1)} %all_to_all.11.shares_ref, f32[1,128]{1,0:T(1,128)S(1)} %get-tuple-element.13.held_log_ref), custom_call_target="tpu_custom_call" | custom-call | tf_op jit(solution)/shard_map/pallas_call | solution.py:197
Async XLA Ops:
  13.8 1.9 %collective-permute-start = (f32[40,128]{1,0:T(8,128)S(1)}, f32[40,128]{1,0:T(8,128)S(1)}, u32[]{:S(2)}, u32[]{:S(2)}) collective-permute-start(f32[40,128]{1,0:T(8,128)S(1)} %shard_map.60.refs_0_), channel_id=1, source_target_pairs={{0,1},{1,0},{2,3},{3,2},{4,5},{5,4},{6,7},{7,6},{8,9},{9,8},{10,11... | collective-permute-start | bytes 61448 | tf_op jit(solution)/shard_map/ppermute | solution.py:191

commit v11 on v1

--- a/solution.py
+++ b/solution.py
@@ -37,16 +37,10 @@
     return parts[0]
 
 
-def load_kernel(
-    x_ref, bounds_ref, spread_ref, counts_ref,
-    out_ref, held_bounds, held_spread, target_ref,
-    held_x, held_counts, sems,
-):
-    sources = (x_ref, bounds_ref, spread_ref, counts_ref)
-    targets = (held_x, held_bounds, held_spread, held_counts)
+def load_kernel(x_ref, spread_ref, out_ref, held_spread, held_x, sems):
     copies = [
-        pltpu.make_async_copy(source, target, sems.at[i])
-        for i, (source, target) in enumerate(zip(sources, targets))
+        pltpu.make_async_copy(x_ref, held_x, sems.at[0]),
+        pltpu.make_async_copy(spread_ref, held_spread, sems.at[1]),
     ]
     for copy in copies:
         copy.start()
@@ -55,10 +49,7 @@
     packed = jnp.concatenate([held_x[8 * j : 8 * (j + 1), :] for j in range(rows // 8)], axis=1)
     for peer in range(out_ref.shape[0]):
         out_ref[peer] = packed
-    for copy in copies[1:]:
-        copy.wait()
-    smoothing = 1.0 / TABLE_ROWS
-    target_ref[...] = jnp.log(held_counts[...].astype(jnp.float32) / TABLE_ROWS + smoothing)
+    copies[1].wait()
 
 
 def terms_kernel(width, blocks_ref, bounds_ref, spread_ref, out_ref):
@@ -158,14 +149,15 @@
 
 
 def finish_kernel(sample_total, query_total, *refs):
-    part_refs, (target_ref, log_ref, share_ref) = refs[:-3], refs[-3:]
+    part_refs, (counts_ref, log_ref, share_ref) = refs[:-3], refs[-3:]
     whole = tree_sum([ref[...] for ref in part_refs])
     dims, queries = whole.shape[0] - 8, whole.shape[1]
     smoothing = 1.0 / TABLE_ROWS
     estimate = whole[dims : dims + 1] / sample_total
     log_est = jnp.log(estimate + smoothing)
     log_ref[...] = log_est
-    weight = 2.0 * (log_est - target_ref[...]) / (query_total * (estimate + smoothing))
+    target = jnp.log(counts_ref[...].astype(jnp.float32) / TABLE_ROWS + smoothing)
+    weight = 2.0 * (log_est - target) / (query_total * (estimate + smoothing))
     terms = whole[:dims] * (weight / sample_total)
     terms = jnp.concatenate([terms, jnp.zeros((queries - dims, queries), jnp.float32)], axis=0)
     share = jnp.sum(terms.T, axis=0, keepdims=True)
@@ -211,20 +203,17 @@
     sample_total = width * blocks * copies
     query_total = queries * blocks
 
-    counts_vector = pltpu.VMEM((1, queries), jnp.int32)
-    packed, bounds, spread, target = call(
+    packed, spread = call(
         load_kernel,
         [
             pltpu.with_memory_space_constraint(array, pltpu.HBM)
-            for array in (samples, bounds, spread.reshape(1, dims), counts.reshape(1, queries))
+            for array in (samples, spread.reshape(1, dims))
         ],
         [
             pltpu.VMEM((blocks, 8, dims * width // 8), jnp.float32),
-            pltpu.VMEM(bounds.shape, bounds.dtype),
             pltpu.VMEM((1, dims), jnp.float32),
-            pltpu.VMEM((1, queries), jnp.float32),
         ],
-        [pltpu.VMEM((dims, width), jnp.float32), counts_vector, pltpu.SemaphoreType.DMA((4,))],
+        [pltpu.VMEM((dims, width), jnp.float32), pltpu.SemaphoreType.DMA((2,))],
         placed=pl.ANY,
     )
     turned = [1] + [0] * (blocks - 1)
@@ -241,7 +230,7 @@
     )
     log_est, share = call(
         functools.partial(finish_kernel, sample_total, query_total),
-        everyone(part, "grp") + [target],
+        everyone(part, "grp") + [counts.reshape(1, queries)],
         [shape(1, queries), shape(blocks, 1, queries)],
     )
     shares = exchange(share)

time: 25.6 us -> 25.6 us (level)
  no operation moved by 1% of the time
where the time goes in v11:
time: 25.6 us; the launch traced here: 25.1 us
  blocking collectives  20.1 us (79%)
  Pallas kernels  2.46 us (10%)
  starting transfers between devices  1.01 us (4%)
  waiting for transfers between devices  0.84 us (3%)
  between operations  0.67 us (3%)
    all_to_all x2, blocking collectives, on_device(): lax.all_to_all(x, ('blk', 'grp'), 0, 0, axis_index_groups=groups)  20.1 us
    pallas_call x4, Pallas kernels, call(): pl.pallas_call(kernel, out_shape=outs[0] if single else outs, in_specs=[p...  2.46 us
    ppermute x1, starting transfers between devices, everyone(): lax.ppermute(x, axis, [(i, i ^ offset) for i in range(size)])  1.01 us
    ppermute x1, waiting for transfers between devices, everyone(): lax.ppermute(x, axis, [(i, i ^ offset) for i in range(size)])  0.84 us
  transfers between devices with their start and end apart: 1, of which 1 were waited for; matrix products, arithmetic and copies ran while one was open for 0% of the time, Pallas kernels for 0%

profile of v11, /device:TPU:0, one launch (start us, length us, event | category | flops | bytes accessed | tf_op | source)
XLA Modules:
  0.0 25.1 jit_solution(9186996385388167451)
XLA Ops:
  0.6 0.8 %shard_map.59 = (f32[16,8,128]{2,1,0:T(8,128)S(1)}, f32[1,32]{1,0:T(1,128)S(1)}) custom-call(f32[32,32]{1,0:T(8,128)} %x_ref.1, f32[1,32]{1,0:T(1,128)} %bitcast.3), custom_call_target="tpu_custom_call" | custom-call | tf_op jit(solution)/shard_map/pallas_call | solution.py:183
  1.4 0.0 copy-start
  1.5 11.2 %all_to_all.10.blocks_ref = f32[16,8,128]{2,1,0:T(8,128)S(1)} all-to-all(f32[16,8,128]{2,1,0:T(8,128)S(1)} %get-tuple-element.6), channel_id=1, replica_groups={{30,28,26,24,22,20,18,16,14,12,10,8,6,4,2,1},{31,29,27,25,23,21,19,17,1..., dimensions={0} | all-to-all | bytes 131072 | tf_op jit(solution)/shard_map/all_to_all | solution.py:224
  12.7 0.0 copy-done
  12.7 1.0 %shard_map.60.refs_0_ = f32[40,128]{1,0:T(8,128)S(1)} custom-call(f32[16,8,128]{2,1,0:T(8,128)S(1)} %all_to_all.10.blocks_ref, s32[2,32,128]{2,1,0:T(8,128)S(1)} %copy-done, f32[1,32]{1,0:T(1,128)S(1)} %get-tuple-element.7.spread_ref), custom_call_target="tpu_custom_call" | custom-call | tf_op jit(solution)/shard_map/pallas_call | solution.py:183
  13.7 0.0 copy-start.1
  13.7 1.0 %collective-permute-start = (f32[40,128]{1,0:T(8,128)S(1)}, f32[40,128]{1,0:T(8,128)S(1)}, u32[]{:S(2)}, u32[]{:S(2)}) collective-permute-start(f32[40,128]{1,0:T(8,128)S(1)} %shard_map.60.refs_0_), channel_id=1, source_target_pairs={{0,1},{1,0},{2,3},{3,2},{4,5},{5,4},{6,7},{7,6},{8,9},{9,8},{10,11... | collective-permute-start | bytes 61448 | tf_op jit(solution)/shard_map/ppermute | solution.py:177
  14.7 0.8 %collective-permute-done.refs_1_ = f32[40,128]{1,0:T(8,128)S(1)} collective-permute-done((f32[40,128]{1,0:T(8,128)S(1)}, f32[40,128]{1,0:T(8,128)S(1)}, u32[]{:S(2)}, u32[]{:S(2)}) %collective-permute-start) | collective-permute-done | bytes 20512 | tf_op jit(solution)/shard_map/ppermute | solution.py:177
  15.6 0.0 copy-done.1
  15.6 0.1 shard_map.61
  15.7 8.9 %all_to_all.11.shares_ref = f32[16,1,128]{2,1,0:T(1,128)S(1)} all-to-all(f32[16,1,128]{2,1,0:T(1,128)S(1)} %get-tuple-element.8), channel_id=1, replica_groups={{30,28,26,24,22,20,18,16,14,12,10,8,6,4,2,1},{31,29,27,25,23,21,19,17,1..., dimensions={0} | all-to-all | bytes 16384 | tf_op jit(solution)/shard_map/all_to_all | solution.py:224
  24.6 0.5 %shard_map.62 = (f32[128]{0:T(128)}, f32[32]{0:T(128)}) custom-call(f32[16,1,128]{2,1,0:T(1,128)S(1)} %all_to_all.11.shares_ref, f32[1,128]{1,0:T(1,128)S(1)} %get-tuple-element.9.held_log_ref), custom_call_target="tpu_custom_call" | custom-call | tf_op jit(solution)/shard_map/pallas_call | solution.py:183
Async XLA Ops:
  1.4 11.2 %copy-start = (s32[2,32,128]{2,1,0:T(8,128)S(1)}, s32[2,32,128]{2,1,0:T(8,128)}, u32[]{:S(2)}) copy-start(s32[2,32,128]{2,1,0:T(8,128)} %bounds_ref.1) | copy-start | bytes 98308
  13.7 1.9 %copy-start.1 = (s32[128]{0:T(128)S(1)}, s32[128]{0:T(128)}, u32[]{:S(2)}) copy-start(s32[128]{0:T(128)} %param.7) | copy-start | bytes 1540
  13.7 1.9 %collective-permute-start = (f32[40,128]{1,0:T(8,128)S(1)}, f32[40,128]{1,0:T(8,128)S(1)}, u32[]{:S(2)}, u32[]{:S(2)}) collective-permute-start(f32[40,128]{1,0:T(8,128)S(1)} %shard_map.60.refs_0_), channel_id=1, source_target_pairs={{0,1},{1,0},{2,3},{3,2},{4,5},{5,4},{6,7},{7,6},{8,9},{9,8},{10,11... | collective-permute-start | bytes 61448 | tf_op jit(solution)/shard_map/ppermute | solution.py:177

commit v12 on v11

--- a/solution.py
+++ b/solution.py
@@ -217,8 +217,10 @@
         placed=pl.ANY,
     )
     turned = [1] + [0] * (blocks - 1)
+    hops = lambda b: (b & 1) + (b >> 1 & 1) + (b >> 2)
+    order = sorted(range(blocks), key=lambda b: (-hops(b), -b))
     groups = [
-        [b * copies + (c + turned[b]) % copies for b in reversed(range(blocks))]
+        [b * copies + (c + turned[b]) % copies for b in order]
         for c in range(copies)
     ]
     exchange = lambda x: lax.all_to_all(x, ("blk", "grp"), 0, 0, axis_index_groups=groups)

time: 25.6 us -> 25.5 us (level)
  no operation moved by 1% of the time
where the time goes in v12:
time: 25.5 us; the launch traced here: 25 us
  blocking collectives  20 us (78%)
  Pallas kernels  2.46 us (10%)
  starting transfers between devices  1.02 us (4%)
  waiting for transfers between devices  0.84 us (3%)
  between operations  0.67 us (3%)
    all_to_all x2, blocking collectives, on_device(): lax.all_to_all(x, ('blk', 'grp'), 0, 0, axis_index_groups=groups)  20 us
    pallas_call x4, Pallas kernels, call(): pl.pallas_call(kernel, out_shape=outs[0] if single else outs, in_specs=[p...  2.46 us
    ppermute x1, starting transfers between devices, everyone(): lax.ppermute(x, axis, [(i, i ^ offset) for i in range(size)])  1.02 us
    ppermute x1, waiting for transfers between devices, everyone(): lax.ppermute(x, axis, [(i, i ^ offset) for i in range(size)])  0.84 us
  transfers between devices with their start and end apart: 1, of which 1 were waited for; matrix products, arithmetic and copies ran while one was open for 0% of the time, Pallas kernels for 0%

profile of v12, /device:TPU:0, one launch (start us, length us, event | category | flops | bytes accessed | tf_op | source)
XLA Modules:
  0.0 25.0 jit_solution(5864661064824102131)
XLA Ops:
  0.6 0.8 %shard_map.59 = (f32[16,8,128]{2,1,0:T(8,128)S(1)}, f32[1,32]{1,0:T(1,128)S(1)}) custom-call(f32[32,32]{1,0:T(8,128)} %x_ref.1, f32[1,32]{1,0:T(1,128)} %bitcast.3), custom_call_target="tpu_custom_call" | custom-call | tf_op jit(solution)/shard_map/pallas_call | solution.py:183
  1.4 0.0 copy-start
  1.5 11.2 %all_to_all.10.blocks_ref = f32[16,8,128]{2,1,0:T(8,128)S(1)} all-to-all(f32[16,8,128]{2,1,0:T(8,128)S(1)} %get-tuple-element.6), channel_id=1, replica_groups={{30,28,26,22,24,20,18,14,16,12,10,6,8,4,2,1},{31,29,27,23,25,21,19,15,1..., dimensions={0} | all-to-all | bytes 131072 | tf_op jit(solution)/shard_map/all_to_all | solution.py:226
  12.7 0.0 copy-done
  12.7 1.0 %shard_map.60.refs_0_ = f32[40,128]{1,0:T(8,128)S(1)} custom-call(f32[16,8,128]{2,1,0:T(8,128)S(1)} %all_to_all.10.blocks_ref, s32[2,32,128]{2,1,0:T(8,128)S(1)} %copy-done, f32[1,32]{1,0:T(1,128)S(1)} %get-tuple-element.7.spread_ref), custom_call_target="tpu_custom_call" | custom-call | tf_op jit(solution)/shard_map/pallas_call | solution.py:183
  13.7 0.0 copy-start.1
  13.7 1.0 %collective-permute-start = (f32[40,128]{1,0:T(8,128)S(1)}, f32[40,128]{1,0:T(8,128)S(1)}, u32[]{:S(2)}, u32[]{:S(2)}) collective-permute-start(f32[40,128]{1,0:T(8,128)S(1)} %shard_map.60.refs_0_), channel_id=1, source_target_pairs={{0,1},{1,0},{2,3},{3,2},{4,5},{5,4},{6,7},{7,6},{8,9},{9,8},{10,11... | collective-permute-start | bytes 61448 | tf_op jit(solution)/shard_map/ppermute | solution.py:177
  14.8 0.8 %collective-permute-done.refs_1_ = f32[40,128]{1,0:T(8,128)S(1)} collective-permute-done((f32[40,128]{1,0:T(8,128)S(1)}, f32[40,128]{1,0:T(8,128)S(1)}, u32[]{:S(2)}, u32[]{:S(2)}) %collective-permute-start) | collective-permute-done | bytes 20512 | tf_op jit(solution)/shard_map/ppermute | solution.py:177
  15.6 0.0 copy-done.1
  15.6 0.1 shard_map.61
  15.7 8.8 %all_to_all.11.shares_ref = f32[16,1,128]{2,1,0:T(1,128)S(1)} all-to-all(f32[16,1,128]{2,1,0:T(1,128)S(1)} %get-tuple-element.8), channel_id=1, replica_groups={{30,28,26,22,24,20,18,14,16,12,10,6,8,4,2,1},{31,29,27,23,25,21,19,15,1..., dimensions={0} | all-to-all | bytes 16384 | tf_op jit(solution)/shard_map/all_to_all | solution.py:226
  24.5 0.5 %shard_map.62 = (f32[128]{0:T(128)}, f32[32]{0:T(128)}) custom-call(f32[16,1,128]{2,1,0:T(1,128)S(1)} %all_to_all.11.shares_ref, f32[1,128]{1,0:T(1,128)S(1)} %get-tuple-element.9.held_log_ref), custom_call_target="tpu_custom_call" | custom-call | tf_op jit(solution)/shard_map/pallas_call | solution.py:183
Async XLA Ops:
  1.4 11.3 %copy-start = (s32[2,32,128]{2,1,0:T(8,128)S(1)}, s32[2,32,128]{2,1,0:T(8,128)}, u32[]{:S(2)}) copy-start(s32[2,32,128]{2,1,0:T(8,128)} %bounds_ref.1) | copy-start | bytes 98308
  13.7 1.9 %copy-start.1 = (s32[128]{0:T(128)S(1)}, s32[128]{0:T(128)}, u32[]{:S(2)}) copy-start(s32[128]{0:T(128)} %param.7) | copy-start | bytes 1540
  13.7 1.9 %collective-permute-start = (f32[40,128]{1,0:T(8,128)S(1)}, f32[40,128]{1,0:T(8,128)S(1)}, u32[]{:S(2)}, u32[]{:S(2)}) collective-permute-start(f32[40,128]{1,0:T(8,128)S(1)} %shard_map.60.refs_0_), channel_id=1, source_target_pairs={{0,1},{1,0},{2,3},{3,2},{4,5},{5,4},{6,7},{7,6},{8,9},{9,8},{10,11... | collective-permute-start | bytes 61448 | tf_op jit(solution)/shard_map/ppermute | solution.py:177

commit v13 on v12

--- a/solution.py
+++ b/solution.py
@@ -121,7 +121,9 @@
         )
         inside = []
         for at_row in range(0, per_piece * width, 16):
-            whole, sums = step(picked[at_row : at_row + 16], sums)
+            upper, sums = step(picked[at_row : at_row + 8], sums)
+            lower, sums = step(picked[at_row + 8 : at_row + 16], sums)
+            whole = jnp.concatenate([upper, lower], axis=0)
             inside.append(jnp.concatenate(split(whole, 2), axis=1))
         inside = jnp.concatenate(inside, axis=0)
         products = products + jnp.dot(ratio, inside, preferred_element_type=jnp.float32)
@@ -132,7 +134,7 @@
             totals = piece(number * group + start, totals)
         return totals
 
-    zero = jnp.zeros((16, queries), jnp.float32)
+    zero = jnp.zeros((8, queries), jnp.float32)
     totals = (zero,) * (1 + LIMITED) + (jnp.zeros((2 * dims, 2 * queries), jnp.float32),)
     if count == group:
         totals = pieces(0, totals)

time: 25.5 us -> 25.5 us (level)
  no operation moved by 1% of the time
where the time goes in v13:
time: 25.5 us; the launch traced here: 25 us
  blocking collectives  20 us (78%)
  Pallas kernels  2.45 us (10%)
  starting transfers between devices  1.02 us (4%)
  waiting for transfers between devices  0.84 us (3%)
  between operations  0.67 us (3%)
    all_to_all x2, blocking collectives, on_device(): lax.all_to_all(x, ('blk', 'grp'), 0, 0, axis_index_groups=groups)  20 us
    pallas_call x4, Pallas kernels, call(): pl.pallas_call(kernel, out_shape=outs[0] if single else outs, in_specs=[p...  2.45 us
    ppermute x1, starting transfers between devices, everyone(): lax.ppermute(x, axis, [(i, i ^ offset) for i in range(size)])  1.02 us
    ppermute x1, waiting for transfers between devices, everyone(): lax.ppermute(x, axis, [(i, i ^ offset) for i in range(size)])  0.84 us
  transfers between devices with their start and end apart: 1, of which 1 were waited for; matrix products, arithmetic and copies ran while one was open for 0% of the time, Pallas kernels for 0%

profile of v13, /device:TPU:0, one launch (start us, length us, event | category | flops | bytes accessed | tf_op | source)
XLA Modules:
  0.0 25.0 jit_solution(8885816463590609278)
XLA Ops:
  0.6 0.8 %shard_map.59 = (f32[16,8,128]{2,1,0:T(8,128)S(1)}, f32[1,32]{1,0:T(1,128)S(1)}) custom-call(f32[32,32]{1,0:T(8,128)} %x_ref.1, f32[1,32]{1,0:T(1,128)} %bitcast.3), custom_call_target="tpu_custom_call" | custom-call | tf_op jit(solution)/shard_map/pallas_call | solution.py:185
  1.4 0.0 copy-start
  1.5 11.2 %all_to_all.10.blocks_ref = f32[16,8,128]{2,1,0:T(8,128)S(1)} all-to-all(f32[16,8,128]{2,1,0:T(8,128)S(1)} %get-tuple-element.6), channel_id=1, replica_groups={{30,28,26,22,24,20,18,14,16,12,10,6,8,4,2,1},{31,29,27,23,25,21,19,15,1..., dimensions={0} | all-to-all | bytes 131072 | tf_op jit(solution)/shard_map/all_to_all | solution.py:228
  12.7 0.0 copy-done
  12.7 1.0 %shard_map.60.refs_0_ = f32[40,128]{1,0:T(8,128)S(1)} custom-call(f32[16,8,128]{2,1,0:T(8,128)S(1)} %all_to_all.10.blocks_ref, s32[2,32,128]{2,1,0:T(8,128)S(1)} %copy-done, f32[1,32]{1,0:T(1,128)S(1)} %get-tuple-element.7.spread_ref), custom_call_target="tpu_custom_call" | custom-call | tf_op jit(solution)/shard_map/pallas_call | solution.py:185
  13.7 0.0 copy-start.1
  13.7 1.0 %collective-permute-start = (f32[40,128]{1,0:T(8,128)S(1)}, f32[40,128]{1,0:T(8,128)S(1)}, u32[]{:S(2)}, u32[]{:S(2)}) collective-permute-start(f32[40,128]{1,0:T(8,128)S(1)} %shard_map.60.refs_0_), channel_id=1, source_target_pairs={{0,1},{1,0},{2,3},{3,2},{4,5},{5,4},{6,7},{7,6},{8,9},{9,8},{10,11... | collective-permute-start | bytes 61448 | tf_op jit(solution)/shard_map/ppermute | solution.py:179
  14.7 0.8 %collective-permute-done.refs_1_ = f32[40,128]{1,0:T(8,128)S(1)} collective-permute-done((f32[40,128]{1,0:T(8,128)S(1)}, f32[40,128]{1,0:T(8,128)S(1)}, u32[]{:S(2)}, u32[]{:S(2)}) %collective-permute-start) | collective-permute-done | bytes 20512 | tf_op jit(solution)/shard_map/ppermute | solution.py:179
  15.6 0.0 copy-done.1
  15.6 0.1 shard_map.61
  15.7 8.8 %all_to_all.11.shares_ref = f32[16,1,128]{2,1,0:T(1,128)S(1)} all-to-all(f32[16,1,128]{2,1,0:T(1,128)S(1)} %get-tuple-element.8), channel_id=1, replica_groups={{30,28,26,22,24,20,18,14,16,12,10,6,8,4,2,1},{31,29,27,23,25,21,19,15,1..., dimensions={0} | all-to-all | bytes 16384 | tf_op jit(solution)/shard_map/all_to_all | solution.py:228
  24.5 0.5 %shard_map.62 = (f32[128]{0:T(128)}, f32[32]{0:T(128)}) custom-call(f32[16,1,128]{2,1,0:T(1,128)S(1)} %all_to_all.11.shares_ref, f32[1,128]{1,0:T(1,128)S(1)} %get-tuple-element.9.held_log_ref), custom_call_target="tpu_custom_call" | custom-call | tf_op jit(solution)/shard_map/pallas_call | solution.py:185
Async XLA Ops:
  1.4 11.3 %copy-start = (s32[2,32,128]{2,1,0:T(8,128)S(1)}, s32[2,32,128]{2,1,0:T(8,128)}, u32[]{:S(2)}) copy-start(s32[2,32,128]{2,1,0:T(8,128)} %bounds_ref.1) | copy-start | bytes 98308
  13.7 1.9 %copy-start.1 = (s32[128]{0:T(128)S(1)}, s32[128]{0:T(128)}, u32[]{:S(2)}) copy-start(s32[128]{0:T(128)} %param.7) | copy-start | bytes 1540
  13.7 1.9 %collective-permute-start = (f32[40,128]{1,0:T(8,128)S(1)}, f32[40,128]{1,0:T(8,128)S(1)}, u32[]{:S(2)}, u32[]{:S(2)}) collective-permute-start(f32[40,128]{1,0:T(8,128)S(1)} %shard_map.60.refs_0_), channel_id=1, source_target_pairs={{0,1},{1,0},{2,3},{3,2},{4,5},{5,4},{6,7},{7,6},{8,9},{9,8},{10,11... | collective-permute-start | bytes 61448 | tf_op jit(solution)/shard_map/ppermute | solution.py:179

commit v14 on v13

--- a/solution.py
+++ b/solution.py
@@ -161,8 +161,8 @@
     target = jnp.log(counts_ref[...].astype(jnp.float32) / TABLE_ROWS + smoothing)
     weight = 2.0 * (log_est - target) / (query_total * (estimate + smoothing))
     terms = whole[:dims] * (weight / sample_total)
-    terms = jnp.concatenate([terms, jnp.zeros((queries - dims, queries), jnp.float32)], axis=0)
     share = jnp.sum(terms.T, axis=0, keepdims=True)
+    share = jnp.concatenate([share, jnp.zeros((1, queries - dims), jnp.float32)], axis=1)
     for peer in range(share_ref.shape[0]):
         share_ref[peer] = share
 

time: 25.5 us -> 25.5 us (level)
  no operation moved by 1% of the time
where the time goes in v14:
time: 25.5 us; the launch traced here: 25 us
  blocking collectives  20 us (78%)
  Pallas kernels  2.45 us (10%)
  starting transfers between devices  1.02 us (4%)
  waiting for transfers between devices  0.84 us (3%)
  between operations  0.67 us (3%)
    all_to_all x2, blocking collectives, on_device(): lax.all_to_all(x, ('blk', 'grp'), 0, 0, axis_index_groups=groups)  20 us
    pallas_call x4, Pallas kernels, call(): pl.pallas_call(kernel, out_shape=outs[0] if single else outs, in_specs=[p...  2.45 us
    ppermute x1, starting transfers between devices, everyone(): lax.ppermute(x, axis, [(i, i ^ offset) for i in range(size)])  1.02 us
    ppermute x1, waiting for transfers between devices, everyone(): lax.ppermute(x, axis, [(i, i ^ offset) for i in range(size)])  0.84 us
  transfers between devices with their start and end apart: 1, of which 1 were waited for; matrix products, arithmetic and copies ran while one was open for 0% of the time, Pallas kernels for 0%

profile of v14, /device:TPU:0, one launch (start us, length us, event | category | flops | bytes accessed | tf_op | source)
XLA Modules:
  0.0 25.0 jit_solution(5819337420446473293)
XLA Ops:
  0.6 0.8 %shard_map.59 = (f32[16,8,128]{2,1,0:T(8,128)S(1)}, f32[1,32]{1,0:T(1,128)S(1)}) custom-call(f32[32,32]{1,0:T(8,128)} %x_ref.1, f32[1,32]{1,0:T(1,128)} %bitcast.3), custom_call_target="tpu_custom_call" | custom-call | tf_op jit(solution)/shard_map/pallas_call | solution.py:185
  1.4 0.0 copy-start
  1.5 11.2 %all_to_all.10.blocks_ref = f32[16,8,128]{2,1,0:T(8,128)S(1)} all-to-all(f32[16,8,128]{2,1,0:T(8,128)S(1)} %get-tuple-element.6), channel_id=1, replica_groups={{30,28,26,22,24,20,18,14,16,12,10,6,8,4,2,1},{31,29,27,23,25,21,19,15,1..., dimensions={0} | all-to-all | bytes 131072 | tf_op jit(solution)/shard_map/all_to_all | solution.py:228
  12.7 0.0 copy-done
  12.7 1.0 %shard_map.60.refs_0_ = f32[40,128]{1,0:T(8,128)S(1)} custom-call(f32[16,8,128]{2,1,0:T(8,128)S(1)} %all_to_all.10.blocks_ref, s32[2,32,128]{2,1,0:T(8,128)S(1)} %copy-done, f32[1,32]{1,0:T(1,128)S(1)} %get-tuple-element.7.spread_ref), custom_call_target="tpu_custom_call" | custom-call | tf_op jit(solution)/shard_map/pallas_call | solution.py:185
  13.7 0.0 copy-start.1
  13.7 1.0 %collective-permute-start = (f32[40,128]{1,0:T(8,128)S(1)}, f32[40,128]{1,0:T(8,128)S(1)}, u32[]{:S(2)}, u32[]{:S(2)}) collective-permute-start(f32[40,128]{1,0:T(8,128)S(1)} %shard_map.60.refs_0_), channel_id=1, source_target_pairs={{0,1},{1,0},{2,3},{3,2},{4,5},{5,4},{6,7},{7,6},{8,9},{9,8},{10,11... | collective-permute-start | bytes 61448 | tf_op jit(solution)/shard_map/ppermute | solution.py:179
  14.7 0.8 %collective-permute-done.refs_1_ = f32[40,128]{1,0:T(8,128)S(1)} collective-permute-done((f32[40,128]{1,0:T(8,128)S(1)}, f32[40,128]{1,0:T(8,128)S(1)}, u32[]{:S(2)}, u32[]{:S(2)}) %collective-permute-start) | collective-permute-done | bytes 20512 | tf_op jit(solution)/shard_map/ppermute | solution.py:179
  15.6 0.0 copy-done.1
  15.6 0.1 shard_map.61
  15.7 8.8 %all_to_all.11.shares_ref = f32[16,1,128]{2,1,0:T(1,128)S(1)} all-to-all(f32[16,1,128]{2,1,0:T(1,128)S(1)} %get-tuple-element.8), channel_id=1, replica_groups={{30,28,26,22,24,20,18,14,16,12,10,6,8,4,2,1},{31,29,27,23,25,21,19,15,1..., dimensions={0} | all-to-all | bytes 16384 | tf_op jit(solution)/shard_map/all_to_all | solution.py:228
  24.5 0.5 %shard_map.62 = (f32[128]{0:T(128)}, f32[32]{0:T(128)}) custom-call(f32[16,1,128]{2,1,0:T(1,128)S(1)} %all_to_all.11.shares_ref, f32[1,128]{1,0:T(1,128)S(1)} %get-tuple-element.9.held_log_ref), custom_call_target="tpu_custom_call" | custom-call | tf_op jit(solution)/shard_map/pallas_call | solution.py:185
Async XLA Ops:
  1.4 11.3 %copy-start = (s32[2,32,128]{2,1,0:T(8,128)S(1)}, s32[2,32,128]{2,1,0:T(8,128)}, u32[]{:S(2)}) copy-start(s32[2,32,128]{2,1,0:T(8,128)} %bounds_ref.1) | copy-start | bytes 98308
  13.7 1.9 %copy-start.1 = (s32[128]{0:T(128)S(1)}, s32[128]{0:T(128)}, u32[]{:S(2)}) copy-start(s32[128]{0:T(128)} %param.7) | copy-start | bytes 1540
  13.7 1.9 %collective-permute-start = (f32[40,128]{1,0:T(8,128)S(1)}, f32[40,128]{1,0:T(8,128)S(1)}, u32[]{:S(2)}, u32[]{:S(2)}) collective-permute-start(f32[40,128]{1,0:T(8,128)S(1)} %shard_map.60.refs_0_), channel_id=1, source_target_pairs={{0,1},{1,0},{2,3},{3,2},{4,5},{5,4},{6,7},{7,6},{8,9},{9,8},{10,11... | collective-permute-start | bytes 61448 | tf_op jit(solution)/shard_map/ppermute | solution.py:179

commit v15 on v12

--- a/solution.py
+++ b/solution.py
@@ -38,18 +38,22 @@
 
 
 def load_kernel(x_ref, spread_ref, out_ref, held_spread, held_x, sems):
+    bands = [pl.ds(8 * j, 8) for j in range(held_x.shape[0] // 8)]
     copies = [
-        pltpu.make_async_copy(x_ref, held_x, sems.at[0]),
-        pltpu.make_async_copy(spread_ref, held_spread, sems.at[1]),
+        pltpu.make_async_copy(x_ref.at[band], held_x.at[band], sems.at[j])
+        for j, band in enumerate(bands)
     ]
+    copies.append(pltpu.make_async_copy(spread_ref, held_spread, sems.at[len(bands)]))
     for copy in copies:
         copy.start()
-    copies[0].wait()
-    rows = held_x.shape[0]
-    packed = jnp.concatenate([held_x[8 * j : 8 * (j + 1), :] for j in range(rows // 8)], axis=1)
+    pieces = []
+    for copy, band in zip(copies, bands):
+        copy.wait()
+        pieces.append(held_x[band, :])
+    packed = jnp.concatenate(pieces, axis=1)
     for peer in range(out_ref.shape[0]):
         out_ref[peer] = packed
-    copies[1].wait()
+    copies[-1].wait()
 
 
 def terms_kernel(width, blocks_ref, bounds_ref, spread_ref, out_ref):
@@ -213,7 +217,7 @@
             pltpu.VMEM((blocks, 8, dims * width // 8), jnp.float32),
             pltpu.VMEM((1, dims), jnp.float32),
         ],
-        [pltpu.VMEM((dims, width), jnp.float32), pltpu.SemaphoreType.DMA((2,))],
+        [pltpu.VMEM((dims, width), jnp.float32), pltpu.SemaphoreType.DMA((dims // 8 + 1,))],
         placed=pl.ANY,
     )
     turned = [1] + [0] * (blocks - 1)

time: 25.5 us -> 25.5 us (level)
  no operation moved by 1% of the time
where the time goes in v15:
time: 25.5 us; the launch traced here: 25.1 us
  blocking collectives  20 us (78%)
  Pallas kernels  2.51 us (10%)
  starting transfers between devices  1.02 us (4%)
  waiting for transfers between devices  0.84 us (3%)
  between operations  0.67 us (3%)
    all_to_all x2, blocking collectives, on_device(): lax.all_to_all(x, ('blk', 'grp'), 0, 0, axis_index_groups=groups)  20 us
    pallas_call x4, Pallas kernels, call(): pl.pallas_call(kernel, out_shape=outs[0] if single else outs, in_specs=[p...  2.51 us
    ppermute x1, starting transfers between devices, everyone(): lax.ppermute(x, axis, [(i, i ^ offset) for i in range(size)])  1.02 us
    ppermute x1, waiting for transfers between devices, everyone(): lax.ppermute(x, axis, [(i, i ^ offset) for i in range(size)])  0.84 us
  transfers between devices with their start and end apart: 1, of which 1 were waited for; matrix products, arithmetic and copies ran while one was open for 0% of the time, Pallas kernels for 0%

profile of v15, /device:TPU:0, one launch (start us, length us, event | category | flops | bytes accessed | tf_op | source)
XLA Modules:
  0.0 25.1 jit_solution(14893769223204255698)
XLA Ops:
  0.6 0.9 %shard_map.59 = (f32[16,8,128]{2,1,0:T(8,128)S(1)}, f32[1,32]{1,0:T(1,128)S(1)}) custom-call(f32[32,32]{1,0:T(8,128)} %x_ref.1, f32[1,32]{1,0:T(1,128)} %bitcast.3), custom_call_target="tpu_custom_call" | custom-call | tf_op jit(solution)/shard_map/pallas_call | solution.py:187
  1.5 0.0 copy-start
  1.5 11.2 %all_to_all.10.blocks_ref = f32[16,8,128]{2,1,0:T(8,128)S(1)} all-to-all(f32[16,8,128]{2,1,0:T(8,128)S(1)} %get-tuple-element.6), channel_id=1, replica_groups={{30,28,26,22,24,20,18,14,16,12,10,6,8,4,2,1},{31,29,27,23,25,21,19,15,1..., dimensions={0} | all-to-all | bytes 131072 | tf_op jit(solution)/shard_map/all_to_all | solution.py:230
  12.7 0.0 copy-done
  12.7 1.0 %shard_map.60.refs_0_ = f32[40,128]{1,0:T(8,128)S(1)} custom-call(f32[16,8,128]{2,1,0:T(8,128)S(1)} %all_to_all.10.blocks_ref, s32[2,32,128]{2,1,0:T(8,128)S(1)} %copy-done, f32[1,32]{1,0:T(1,128)S(1)} %get-tuple-element.7.spread_ref), custom_call_target="tpu_custom_call" | custom-call | tf_op jit(solution)/shard_map/pallas_call | solution.py:187
  13.8 0.0 copy-start.1
  13.8 1.0 %collective-permute-start = (f32[40,128]{1,0:T(8,128)S(1)}, f32[40,128]{1,0:T(8,128)S(1)}, u32[]{:S(2)}, u32[]{:S(2)}) collective-permute-start(f32[40,128]{1,0:T(8,128)S(1)} %shard_map.60.refs_0_), channel_id=1, source_target_pairs={{0,1},{1,0},{2,3},{3,2},{4,5},{5,4},{6,7},{7,6},{8,9},{9,8},{10,11... | collective-permute-start | bytes 61448 | tf_op jit(solution)/shard_map/ppermute | solution.py:181
  14.8 0.8 %collective-permute-done.refs_1_ = f32[40,128]{1,0:T(8,128)S(1)} collective-permute-done((f32[40,128]{1,0:T(8,128)S(1)}, f32[40,128]{1,0:T(8,128)S(1)}, u32[]{:S(2)}, u32[]{:S(2)}) %collective-permute-start) | collective-permute-done | bytes 20512 | tf_op jit(solution)/shard_map/ppermute | solution.py:181
  15.6 0.0 copy-done.1
  15.6 0.1 shard_map.61
  15.8 8.8 %all_to_all.11.shares_ref = f32[16,1,128]{2,1,0:T(1,128)S(1)} all-to-all(f32[16,1,128]{2,1,0:T(1,128)S(1)} %get-tuple-element.8), channel_id=1, replica_groups={{30,28,26,22,24,20,18,14,16,12,10,6,8,4,2,1},{31,29,27,23,25,21,19,15,1..., dimensions={0} | all-to-all | bytes 16384 | tf_op jit(solution)/shard_map/all_to_all | solution.py:230
  24.5 0.5 %shard_map.62 = (f32[128]{0:T(128)}, f32[32]{0:T(128)}) custom-call(f32[16,1,128]{2,1,0:T(1,128)S(1)} %all_to_all.11.shares_ref, f32[1,128]{1,0:T(1,128)S(1)} %get-tuple-element.9.held_log_ref), custom_call_target="tpu_custom_call" | custom-call | tf_op jit(solution)/shard_map/pallas_call | solution.py:187
Async XLA Ops:
  1.5 11.3 %copy-start = (s32[2,32,128]{2,1,0:T(8,128)S(1)}, s32[2,32,128]{2,1,0:T(8,128)}, u32[]{:S(2)}) copy-start(s32[2,32,128]{2,1,0:T(8,128)} %bounds_ref.1) | copy-start | bytes 98308
  13.8 1.9 %copy-start.1 = (s32[128]{0:T(128)S(1)}, s32[128]{0:T(128)}, u32[]{:S(2)}) copy-start(s32[128]{0:T(128)} %param.7) | copy-start | bytes 1540
  13.8 1.9 %collective-permute-start = (f32[40,128]{1,0:T(8,128)S(1)}, f32[40,128]{1,0:T(8,128)S(1)}, u32[]{:S(2)}, u32[]{:S(2)}) collective-permute-start(f32[40,128]{1,0:T(8,128)S(1)} %shard_map.60.refs_0_), channel_id=1, source_target_pairs={{0,1},{1,0},{2,3},{3,2},{4,5},{5,4},{6,7},{7,6},{8,9},{9,8},{10,11... | collective-permute-start | bytes 61448 | tf_op jit(solution)/shard_map/ppermute | solution.py:181

commit v16 on v12

--- a/solution.py
+++ b/solution.py
@@ -52,7 +52,15 @@
     copies[1].wait()
 
 
-def terms_kernel(width, blocks_ref, bounds_ref, spread_ref, out_ref):
+def unit_kernel(spread_ref, unit_ref):
+    dims = spread_ref.shape[1]
+    row = lax.broadcasted_iota(jnp.int32, (dims, dims), 0)
+    column = lax.broadcasted_iota(jnp.int32, (dims, dims), 1)
+    unit = jnp.where(row == column, ROOT_HALF / spread_ref[...], 0.0)
+    unit_ref[...] = jnp.broadcast_to(jnp.sum(unit, axis=1, keepdims=True), unit_ref.shape)
+
+
+def terms_kernel(width, blocks_ref, bounds_ref, unit_ref, out_ref):
     dims, queries = bounds_ref.shape[1:]
     count = blocks_ref.shape[0]
     per_piece = 128 // width
@@ -65,10 +73,7 @@
     last = jnp.max(jnp.where(limited, at, -1), axis=0, keepdims=True)
     chosen = [at == first, limited & (at > first) & (at < last), at == last]
 
-    row = lax.broadcasted_iota(jnp.int32, (dims, dims), 0)
-    column = lax.broadcasted_iota(jnp.int32, (dims, dims), 1)
-    spread = jnp.sum(jnp.where(row == column, spread_ref[...], 0.0), axis=1, keepdims=True)
-    unit = ROOT_HALF / spread
+    unit = unit_ref[...]
 
     pick = lambda mask, values: jnp.sum(jnp.where(mask, values, 0.0), axis=0, keepdims=True)
     low = low.astype(jnp.float32) * unit
@@ -227,7 +232,7 @@
     gathered = exchange(packed)
     part = call(
         functools.partial(terms_kernel, width),
-        [gathered, bounds, spread],
+        [gathered, bounds, call(unit_kernel, [spread], [shape(dims, queries)])],
         [shape(dims + 8, queries)],
     )
     log_est, share = call(

time: 25.5 us -> 27 us (1.059)
  blocking collectives: 20 us -> 8.77 us
  starting transfers between devices: 1.02 us -> 10.8 us
  waiting for transfers between devices: 0.84 us -> 3.13 us
  Pallas kernels: 2.46 us -> 3.16 us
    all_to_all x2 -> x1, blocking collectives: 20 us -> 8.77 us  [on_device(): lax.all_to_all(x, ('blk', 'grp'), 0, 0, axis_index_groups=groups)]
    all_to_all x0 -> x1, starting transfers between devices: none -> 9.76 us  [on_device(): lax.all_to_all(x, ('blk', 'grp'), 0, 0, axis_index_groups=groups)]
    all_to_all x0 -> x1, waiting for transfers between devices: none -> 2.29 us  [on_device(): lax.all_to_all(x, ('blk', 'grp'), 0, 0, axis_index_groups=groups)]
    pallas_call x4 -> x5, Pallas kernels: 2.46 us -> 3.16 us  [call(): pl.pallas_call(kernel, out_shape=outs[0] if single else outs, in_specs=[p...]
  transfers between devices with their start and end apart: 1 -> 2, of which waited for: 1 -> 2; matrix products, arithmetic and copies ran while one was open for 0% -> 0% of each run, Pallas kernels for 0% -> 0%
where the time goes in v16:
time: 27 us; the launch traced here: 26.5 us
  starting transfers between devices  10.8 us (40%)
  blocking collectives  8.77 us (32%)
  Pallas kernels  3.16 us (12%)
  waiting for transfers between devices  3.13 us (12%)
  between operations  0.67 us (2%)
    all_to_all x1, starting transfers between devices, on_device(): lax.all_to_all(x, ('blk', 'grp'), 0, 0, axis_index_groups=groups)  9.76 us
    all_to_all x1, blocking collectives, on_device(): lax.all_to_all(x, ('blk', 'grp'), 0, 0, axis_index_groups=groups)  8.77 us
    pallas_call x5, Pallas kernels, call(): pl.pallas_call(kernel, out_shape=outs[0] if single else outs, in_specs=[p...  3.16 us
    all_to_all x1, waiting for transfers between devices, on_device(): lax.all_to_all(x, ('blk', 'grp'), 0, 0, axis_index_groups=groups)  2.29 us
    ppermute x1, starting transfers between devices, everyone(): lax.ppermute(x, axis, [(i, i ^ offset) for i in range(size)])  1.02 us
    ppermute x1, waiting for transfers between devices, everyone(): lax.ppermute(x, axis, [(i, i ^ offset) for i in range(size)])  0.84 us
  transfers between devices with their start and end apart: 2, of which 2 were waited for; matrix products, arithmetic and copies ran while one was open for 0% of the time, Pallas kernels for 0%

profile of v16, /device:TPU:0, one launch (start us, length us, event | category | flops | bytes accessed | tf_op | source)
XLA Modules:
  0.0 26.5 jit_solution(6225133889044875238)
XLA Ops:
  0.6 1.4 %shard_map.59 = (f32[16,8,128]{2,1,0:T(8,128)}, f32[1,32]{1,0:T(1,128)S(1)}) custom-call(f32[32,32]{1,0:T(8,128)} %x_ref.1, f32[1,32]{1,0:T(1,128)} %bitcast.3), custom_call_target="tpu_custom_call" | custom-call | tf_op jit(solution)/shard_map/pallas_call | solution.py:188
  2.1 0.0 copy-start
  2.1 9.8 %all-to-all-start = ((f32[16,8,128]{2,1,0:T(8,128)}), f32[16,8,128]{2,1,0:T(8,128)S(1)}, u32[]{:S(2)}, u32[]{:S(2)}) async-start(f32[16,8,128]{2,1,0:T(8,128)} %get-tuple-element.6), calls=%async_computation | async-start | bytes 131072 | tf_op jit(solution)/shard_map/all_to_all | solution.py:231
  11.9 0.1 shard_map.60.unit_ref
  11.9 2.3 %all-to-all-done.blocks_ref = f32[16,8,128]{2,1,0:T(8,128)S(1)} async-done(((f32[16,8,128]{2,1,0:T(8,128)}), f32[16,8,128]{2,1,0:T(8,128)S(1)}, u32[]{:S(2)}, u32[]{:S(2)}) %all-to-all-start) | async-done | bytes 65568 | tf_op jit(solution)/shard_map/all_to_all | solution.py:231
  14.2 0.0 copy-done
  14.2 1.0 %shard_map.61.refs_0_ = f32[40,128]{1,0:T(8,128)S(1)} custom-call(f32[16,8,128]{2,1,0:T(8,128)S(1)} %all-to-all-done.blocks_ref, s32[2,32,128]{2,1,0:T(8,128)S(1)} %copy-done, f32[32,128]{1,0:T(8,128)S(1)} %shard_map.60.unit_ref), custom_call_target="tpu_custom_call" | custom-call | tf_op jit(solution)/shard_map/pallas_call | solution.py:188
  15.2 0.0 copy-start.1
  15.2 1.0 %collective-permute-start = (f32[40,128]{1,0:T(8,128)S(1)}, f32[40,128]{1,0:T(8,128)S(1)}, u32[]{:S(2)}, u32[]{:S(2)}) collective-permute-start(f32[40,128]{1,0:T(8,128)S(1)} %shard_map.61.refs_0_), channel_id=1, source_target_pairs={{0,1},{1,0},{2,3},{3,2},{4,5},{5,4},{6,7},{7,6},{8,9},{9,8},{10,11... | collective-permute-start | bytes 61448 | tf_op jit(solution)/shard_map/ppermute | solution.py:182
  16.3 0.8 %collective-permute-done.refs_1_ = f32[40,128]{1,0:T(8,128)S(1)} collective-permute-done((f32[40,128]{1,0:T(8,128)S(1)}, f32[40,128]{1,0:T(8,128)S(1)}, u32[]{:S(2)}, u32[]{:S(2)}) %collective-permute-start) | collective-permute-done | bytes 20512 | tf_op jit(solution)/shard_map/ppermute | solution.py:182
  17.1 0.0 copy-done.1
  17.1 0.1 shard_map.62
  17.2 8.8 %all_to_all.10.shares_ref = f32[16,1,128]{2,1,0:T(1,128)S(1)} all-to-all(f32[16,1,128]{2,1,0:T(1,128)S(1)} %get-tuple-element.8), channel_id=1, replica_groups={{30,28,26,22,24,20,18,14,16,12,10,6,8,4,2,1},{31,29,27,23,25,21,19,15,1..., dimensions={0} | all-to-all | bytes 16384 | tf_op jit(solution)/shard_map/all_to_all | solution.py:231
  26.0 0.5 %shard_map.63 = (f32[128]{0:T(128)}, f32[32]{0:T(128)}) custom-call(f32[16,1,128]{2,1,0:T(1,128)S(1)} %all_to_all.10.shares_ref, f32[1,128]{1,0:T(1,128)S(1)} %get-tuple-element.9.held_log_ref), custom_call_target="tpu_custom_call" | custom-call | tf_op jit(solution)/shard_map/pallas_call | solution.py:188
Async XLA Ops:
  2.1 12.1 %copy-start = (s32[2,32,128]{2,1,0:T(8,128)S(1)}, s32[2,32,128]{2,1,0:T(8,128)}, u32[]{:S(2)}) copy-start(s32[2,32,128]{2,1,0:T(8,128)} %bounds_ref.1) | copy-start | bytes 98308
  2.1 12.1 %all-to-all-start = ((f32[16,8,128]{2,1,0:T(8,128)}), f32[16,8,128]{2,1,0:T(8,128)S(1)}, u32[]{:S(2)}, u32[]{:S(2)}) async-start(f32[16,8,128]{2,1,0:T(8,128)} %get-tuple-element.6), calls=%async_computation | async-start | bytes 131072 | tf_op jit(solution)/shard_map/all_to_all | solution.py:231
  15.2 1.9 %copy-start.1 = (s32[128]{0:T(128)S(1)}, s32[128]{0:T(128)}, u32[]{:S(2)}) copy-start(s32[128]{0:T(128)} %param.7) | copy-start | bytes 1540
  15.2 1.9 %collective-permute-start = (f32[40,128]{1,0:T(8,128)S(1)}, f32[40,128]{1,0:T(8,128)S(1)}, u32[]{:S(2)}, u32[]{:S(2)}) collective-permute-start(f32[40,128]{1,0:T(8,128)S(1)} %shard_map.61.refs_0_), channel_id=1, source_target_pairs={{0,1},{1,0},{2,3},{3,2},{4,5},{5,4},{6,7},{7,6},{8,9},{9,8},{10,11... | collective-permute-start | bytes 61448 | tf_op jit(solution)/shard_map/ppermute | solution.py:182

commit v17 on v1

--- a/solution.py
+++ b/solution.py
@@ -130,7 +130,9 @@
         )
         inside = []
         for at_row in range(0, per_piece * width, 16):
-            whole, sums = step(picked[at_row : at_row + 16], sums)
+            upper, sums = step(picked[at_row : at_row + 8], sums)
+            lower, sums = step(picked[at_row + 8 : at_row + 16], sums)
+            whole = jnp.concatenate([upper, lower], axis=0)
             inside.append(jnp.concatenate(split(whole, 2), axis=1))
         inside = jnp.concatenate(inside, axis=0)
         products = products + jnp.dot(ratio, inside, preferred_element_type=jnp.float32)
@@ -141,7 +143,7 @@
             totals = piece(number * group + start, totals)
         return totals
 
-    zero = jnp.zeros((16, queries), jnp.float32)
+    zero = jnp.zeros((8, queries), jnp.float32)
     totals = (zero,) * (1 + LIMITED) + (jnp.zeros((2 * dims, 2 * queries), jnp.float32),)
     if count == group:
         totals = pieces(0, totals)

time: 25.6 us -> 25.6 us (level)
  no operation moved by 1% of the time
where the time goes in v17:
time: 25.6 us; the launch traced here: 25.1 us
  blocking collectives  20.1 us (79%)
  Pallas kernels  2.48 us (10%)
  starting transfers between devices  1.01 us (4%)
  waiting for transfers between devices  0.84 us (3%)
  between operations  0.66 us (3%)
    all_to_all x2, blocking collectives, on_device(): lax.all_to_all(x, ('blk', 'grp'), 0, 0, axis_index_groups=groups)  20.1 us
    pallas_call x4, Pallas kernels, call(): pl.pallas_call(kernel, out_shape=outs[0] if single else outs, in_specs=[p...  2.48 us
    ppermute x1, starting transfers between devices, everyone(): lax.ppermute(x, axis, [(i, i ^ offset) for i in range(size)])  1.01 us
    ppermute x1, waiting for transfers between devices, everyone(): lax.ppermute(x, axis, [(i, i ^ offset) for i in range(size)])  0.84 us
  transfers between devices with their start and end apart: 1, of which 1 were waited for; matrix products, arithmetic and copies ran while one was open for 0% of the time, Pallas kernels for 0%

profile of v17, /device:TPU:0, one launch (start us, length us, event | category | flops | bytes accessed | tf_op | source)
XLA Modules:
  0.0 25.1 jit_solution(14702973128494047041)
XLA Ops:
  0.6 0.8 %shard_map.59 = (f32[16,8,128]{2,1,0:T(8,128)S(1)}, s32[2,32,128]{2,1,0:T(8,128)S(1)}, f32[1,32]{1,0:T(1,128)S(1)}, f32[1,128]{1,0:T(1,128)S(1)}) custom-call(f32[32,32]{1,0:T(8,128)} %x_ref.1, s32[2,32,128]{2,1,0:T(8,128)} %bounds_ref.1, f32[1,32]{1,0:T(1,128)} %bitcast.2, s32[1,128]{1,0:T(1,128)} %bitcast.3), custom_call_target="tpu_custom_call" | custom-call | tf_op jit(solution)/shard_map/pallas_call | solution.py:193
  1.5 11.2 %all_to_all.10.blocks_ref = f32[16,8,128]{2,1,0:T(8,128)S(1)} all-to-all(f32[16,8,128]{2,1,0:T(8,128)S(1)} %get-tuple-element.8), channel_id=1, replica_groups={{30,28,26,24,22,20,18,16,14,12,10,8,6,4,2,1},{31,29,27,25,23,21,19,17,1..., dimensions={0} | all-to-all | bytes 131072 | tf_op jit(solution)/shard_map/all_to_all | solution.py:237
  12.7 1.0 %shard_map.60.refs_0_ = f32[40,128]{1,0:T(8,128)S(1)} custom-call(f32[16,8,128]{2,1,0:T(8,128)S(1)} %all_to_all.10.blocks_ref, s32[2,32,128]{2,1,0:T(8,128)S(1)} %get-tuple-element.9.bounds_ref, f32[1,32]{1,0:T(1,128)S(1)} %get-tuple-element.10.spread_ref), custom_call_target="tpu_custom_call" | custom-call | tf_op jit(solution)/shard_map/pallas_call | solution.py:193
  13.7 1.0 %collective-permute-start = (f32[40,128]{1,0:T(8,128)S(1)}, f32[40,128]{1,0:T(8,128)S(1)}, u32[]{:S(2)}, u32[]{:S(2)}) collective-permute-start(f32[40,128]{1,0:T(8,128)S(1)} %shard_map.60.refs_0_), channel_id=1, source_target_pairs={{0,1},{1,0},{2,3},{3,2},{4,5},{5,4},{6,7},{7,6},{8,9},{9,8},{10,11... | collective-permute-start | bytes 61448 | tf_op jit(solution)/shard_map/ppermute | solution.py:187
  14.7 0.8 %collective-permute-done.refs_1_ = f32[40,128]{1,0:T(8,128)S(1)} collective-permute-done((f32[40,128]{1,0:T(8,128)S(1)}, f32[40,128]{1,0:T(8,128)S(1)}, u32[]{:S(2)}, u32[]{:S(2)}) %collective-permute-start) | collective-permute-done | bytes 20512 | tf_op jit(solution)/shard_map/ppermute | solution.py:187
  15.5 0.1 shard_map.61
  15.7 8.9 %all_to_all.11.shares_ref = f32[16,1,128]{2,1,0:T(1,128)S(1)} all-to-all(f32[16,1,128]{2,1,0:T(1,128)S(1)} %get-tuple-element.12), channel_id=1, replica_groups={{30,28,26,24,22,20,18,16,14,12,10,8,6,4,2,1},{31,29,27,25,23,21,19,17,1..., dimensions={0} | all-to-all | bytes 16384 | tf_op jit(solution)/shard_map/all_to_all | solution.py:237
  24.6 0.5 %shard_map.62 = (f32[128]{0:T(128)}, f32[32]{0:T(128)}) custom-call(f32[16,1,128]{2,1,0:T(1,128)S(1)} %all_to_all.11.shares_ref, f32[1,128]{1,0:T(1,128)S(1)} %get-tuple-element.13.held_log_ref), custom_call_target="tpu_custom_call" | custom-call | tf_op jit(solution)/shard_map/pallas_call | solution.py:193
Async XLA Ops:
  13.7 1.9 %collective-permute-start = (f32[40,128]{1,0:T(8,128)S(1)}, f32[40,128]{1,0:T(8,128)S(1)}, u32[]{:S(2)}, u32[]{:S(2)}) collective-permute-start(f32[40,128]{1,0:T(8,128)S(1)} %shard_map.60.refs_0_), channel_id=1, source_target_pairs={{0,1},{1,0},{2,3},{3,2},{4,5},{5,4},{6,7},{7,6},{8,9},{9,8},{10,11... | collective-permute-start | bytes 61448 | tf_op jit(solution)/shard_map/ppermute | solution.py:187
